TPU v7x, 256 devices: a whole 4x4x8 slice. The times are simulated.
256 devices in a mesh: rows: 128 (over z, y, x), rep: 2 (over core).
Axes of the slice: x: 4, y: 4, z: 8, core: 2. Of those that a mesh axis runs over, the one named last changes fastest.
Arguments:
- features: bfloat16 [32768, 128], P(('rows', 'rep')), may hold values from -6 to 6
- tile_counts: int32 [32768, 128, 128], P(('rows', 'rep')), may hold values from 0 to 3, as said below
- tile_row: int32 [32768], P(('rows', 'rep')), may hold values from 0 to 1
- tile_col: int32 [32768], P(('rows', 'rep')), may hold values from 0 to 255, as said below
- label_ids: int32 [16384], P(('rows', 'rep')), may hold values from 0 to 32767, as said below
- cotangent: bfloat16 [32768, 256], P(('rows', 'rep')), may hold values from -6 to 6
- self_weight: bfloat16 [128, 256], replicated, may hold values from -0.5 to 0.5
- neigh_weight: bfloat16 [128, 256], replicated, may hold values from -0.5 to 0.5
Outputs:
- activation: bfloat16 [32768, 256], P(('rows', 'rep'))
- grad_features: float32 [32768, 128], P(('rows', 'rep'))
- grad_self: float32 [128, 256], replicated
- grad_neigh: float32 [128, 256], replicated
Inputs may be any that keep to these rules, and one draw needn't show every extreme that they name: `tile_counts`: edge counts of one tile; most entries are zero. `tile_col`: every tile held by a device of rep index c names a column block of the feature rows of some device of rep index c. On each device, at most 2 tiles name column blocks held by devices of one rows index, and exactly 2 do for some rows index. `label_ids`: the ids of one device's 64 labels are distinct and lie among that device's own feature rows.
All inputs are finite; a program needn't handle non-finite values.
Results may differ from a plain program's by a relative error of at most 0.0053.
Values may be sent and summed in bfloat16 or wider, within the bound.
No kernel may reach another device: no remote copies, remote signals or barrier semaphores. Data moves between devices by JAX's collectives and lax.ppermute only.
A program may use at most 128 MiB of HBM per device.

v0:
```python
import jax
import jax.numpy as jnp
from jax import lax
from jax.sharding import PartitionSpec as P

edge_moment = 14.0 / 96.0


def derivative(preact, masked):
    sigma = jax.nn.sigmoid(preact)
    return (masked.astype(jnp.float32) * sigma * (1.0 + preact * (1.0 - sigma))).astype(
        jnp.bfloat16
    )


def shards(
    features, tile_counts, tile_row, tile_col, label_ids, cotangent, self_weight, neigh_weight
):
    half_rows, width_in = features.shape
    block_size = tile_counts.shape[1]
    tile_total = tile_counts.shape[0]
    rep_count = lax.axis_size("rep")
    row_count = lax.axis_size("rows")
    per_half = half_rows // block_size
    row_blocks = rep_count * per_half
    scale = (edge_moment * tile_total * rep_count * block_size / row_blocks) ** (-0.5)
    gathered = lax.all_gather(features, "rows", axis=0, tiled=True)
    local_col = tile_col // (rep_count * per_half) * per_half + tile_col % per_half
    panels = gathered.reshape(-1, block_size, width_in)[local_col]
    counts = tile_counts.astype(jnp.bfloat16)
    products = jnp.einsum("tij,tjf->tif", counts, panels, preferred_element_type=jnp.float32)
    owner_table = (tile_row[:, None] == jnp.arange(row_blocks, dtype=jnp.int32)[None, :]).astype(
        jnp.float32
    )
    partial_rows = jnp.einsum(
        "tr,tif->rif", owner_table, products, precision=lax.Precision.HIGHEST
    ).reshape(row_blocks * block_size, width_in)
    local_ids = label_ids % half_rows
    label_mask = jnp.any(
        local_ids[:, None] == jnp.arange(half_rows, dtype=jnp.int32)[None, :], axis=0
    )
    masked = cotangent * label_mask[:, None].astype(jnp.bfloat16)
    rep_place = lax.axis_index("rep")
    neighbour_sum = lax.psum(partial_rows, "rep") * scale
    group_feat, group_masked = (
        lax.all_gather(features, "rep", axis=0, tiled=True),
        lax.all_gather(masked, "rep", axis=0, tiled=True),
    )
    neighbour = neighbour_sum.astype(jnp.bfloat16)
    preact = jnp.dot(group_feat, self_weight, preferred_element_type=jnp.float32) + jnp.dot(
        neighbour, neigh_weight, preferred_element_type=jnp.float32
    )
    activation_all = jax.nn.silu(preact).astype(jnp.bfloat16)
    delta_all = derivative(preact, group_masked)
    back = jnp.einsum(
        "nh,fh->nf", delta_all, neigh_weight, preferred_element_type=jnp.float32
    ).astype(jnp.bfloat16)
    activation = lax.dynamic_slice_in_dim(activation_all, rep_place * half_rows, half_rows, 0)
    delta_own = lax.dynamic_slice_in_dim(delta_all, rep_place * half_rows, half_rows, 0)
    neighbour_own = lax.dynamic_slice_in_dim(neighbour, rep_place * half_rows, half_rows, 0)
    self_part = jnp.einsum("nf,nh->fh", features, delta_own, preferred_element_type=jnp.float32)
    neigh_part = jnp.einsum(
        "nf,nh->fh", neighbour_own, delta_own, preferred_element_type=jnp.float32
    )
    self_total, neigh_total = lax.psum((self_part, neigh_part), ("rows", "rep"))
    grad_scale = float(label_ids.shape[0] * row_count * rep_count) ** (-0.5)
    picked = back.reshape(row_blocks, block_size, width_in)[tile_row]
    col_terms = jnp.einsum(
        "tij,tif->tjf", counts, picked, preferred_element_type=jnp.float32
    ).astype(jnp.bfloat16)
    count = half_rows * lax.axis_size("rows")
    block_count = count // block_size
    placing = (local_col[None, :] == jnp.arange(block_count, dtype=jnp.int32)[:, None]).astype(
        jnp.bfloat16
    )
    summed = jnp.einsum("bt,tif->bif", placing, col_terms, preferred_element_type=jnp.float32)
    scattered = lax.psum_scatter(
        summed.reshape(count, width_in), "rows", scatter_dimension=0, tiled=True
    )
    own_term = jnp.einsum("nh,fh->nf", delta_own, self_weight, preferred_element_type=jnp.float32)
    grad_features = own_term + scale * scattered
    return (activation, grad_features, grad_scale * self_total, grad_scale * neigh_total)


def solution(mesh):
    placed = (
        P(("rows", "rep"), None),
        P(("rows", "rep"), None, None),
        P(("rows", "rep")),
        P(("rows", "rep")),
        P(("rows", "rep")),
        P(("rows", "rep"), None),
        P(),
        P(),
    )
    return jax.shard_map(
        shards,
        mesh=mesh,
        in_specs=placed,
        out_specs=(P(("rows", "rep"), None), P(("rows", "rep"), None), P(), P()),
        check_vma=False,
    )
```

profile of v0, /device:TPU:0, one launch (start us, length us, event | category | flops | bytes accessed | tf_op | source)
XLA Modules:
  0.0 1181.8 jit_solution(13858811002854548067)
XLA Ops:
  8.7 2.1 all_gather.9
  12.1 0.9 broadcast_multiply_fusion.2
  13.1 1.0 fusion.22
  14.1 116.1 %all-gather.2.cloned.1.call-done = bf16[16384,128]{1,0:T(8,128)(2,1)} async-done(((bf16[128,128]{1,0:T(8,128)(2,1)}), bf16[16384,128]{1,0:T(8,128)(2,1)}) %all-gather.2.cloned.1.call-update) | async-done | bytes 4194320 | tf_op jit(solution)/shard_map/all_gather | solution.py:27
  130.2 5.2 gather_fusion
  135.4 11.0 convolution_bitcast_fusion
  146.4 9.4 copy.29
  155.7 6.2 fusion.13
  162.7 1.9 all_gather.11
  164.6 23.8 %all-reduce.4.cloned.1.call-done = f32[256,128]{1,0:T(8,128)} async-done(((f32[256,128]{1,0:T(8,128)}), f32[256,128]{1,0:T(8,128)}) %all-reduce.4.cloned.1.call-update) | async-done | bytes 131088 | tf_op jit(solution)/shard_map/psum | solution.py:44
  188.4 0.9 multiply_convert_fusion.1
  189.8 0.9 convolution_bitcast_fusion.1
  190.7 0.9 fusion.6
  191.5 3.0 gather_fusion.1
  194.6 8.2 convert_bitcast_fusion
  202.8 6.7 copy.32
  209.7 3.4 fusion.4
  213.1 8.1 copy.33
  221.9 239.5 %all-reduce.6.cloned.1.call-done = (f32[128,256]{0,1:T(8,128)}, f32[128,256]{0,1:T(8,128)}) async-done(((f32[128,256]{0,1:T(8,128)}, f32[128,256]{0,1:T(8,128)}), (f32[128,256]{0,1:T(8,128)}, f32[128,256]{0,1:T(8,128)})) %all-reduce.6.cloned.1.call-update) | async-done | bytes 262160 | tf_op jit(solution)/shard_map/psum | solution.py:65
  461.4 1.0 broadcast_multiply_fusion
  462.4 0.8 copy.35
  463.1 0.8 copy.36
  463.9 709.8 %reduce-scatter.2.cloned.1.call-done = f32[128,128]{1,0:T(8,128)} async-done(((f32[16384,128]{1,0:T(8,128)}), f32[128,128]{1,0:T(8,128)}) %reduce-scatter.2.cloned.1.call-update) | async-done | bytes 65552 | tf_op jit(solution)/shard_map/reduce_scatter | solution.py:77
  1173.7 1.6 convolution_add_fusion.1
  (27 shorter events, 5.0 us)
Async XLA Ops:
  7.2 182.2 %copy-start = (bf16[128,256]{1,0:T(8,128)(2,1)S(1)}, bf16[128,256]{1,0:T(8,128)(2,1)}, u32[]{:S(2)}) copy-start(bf16[128,256]{1,0:T(8,128)(2,1)} %param.15) | copy-start | bytes 196612
  7.2 123.0 %all-gather.2.cloned.1.call-start = ((), (), s32[]{:S(2)}) async-start(), calls=%async_computation.1 | async-start | bytes 4227072 | tf_op jit(solution)/shard_map/all_gather | solution.py:27
  7.9 180.5 %all-reduce.4.cloned.1.call-start = ((), (), s32[]{:S(2)}) async-start(), calls=%async_computation.2 | async-start | bytes 262144 | tf_op jit(solution)/shard_map/psum | solution.py:44
  146.4 9.4 copy-start.3
  155.7 34.0 %copy-start.1 = (bf16[128,128]{1,0:T(8,128)(2,1)S(1)}, bf16[128,128]{1,0:T(8,128)(2,1)}, u32[]{:S(2)}) copy-start(bf16[128,128]{1,0:T(8,128)(2,1)} %param.8) | copy-start | bytes 98308
  162.6 298.8 %all-reduce.6.cloned.1.call-start = ((), (), s32[]{:S(2)}) async-start(), calls=%async_computation.4 | async-start | bytes 524288 | tf_op jit(solution)/shard_map/psum | solution.py:65
  209.5 964.2 %reduce-scatter.2.cloned.1.call-start = ((), (), s32[]{:S(2)}) async-start(), calls=%async_computation.3 | async-start | bytes 8454144 | tf_op jit(solution)/shard_map/reduce_scatter | solution.py:77
  221.2 952.4 %copy-start.2 = (bf16[128,256]{1,0:T(8,128)(2,1)S(1)}, bf16[128,256]{1,0:T(8,128)(2,1)}, u32[]{:S(2)}) copy-start(bf16[128,256]{1,0:T(8,128)(2,1)} %param.14) | copy-start | bytes 196612
Sparse Core Ops, SparseCore 0:
  11.6 118.5 all-gather.1
  162.7 25.6 all-reduce.3
  209.6 251.7 all-reduce.5
  463.7 709.8 reduce-scatter.1
where the time goes:
time: 1180 us
  waiting for transfers between devices  1090 us (92%)
  local copies, waits for them, and re-layouts  34.6 us (3%)
  matrix products  33.6 us (3%)
  between operations  13.8 us (1%)
    reduce_scatter x1, waiting for transfers between devices, shards(): lax.psum_scatter(summed.reshape(count, width_in), 'rows', scatter_dimensi...  710 us
    psum x1, waiting for transfers between devices, shards(): self_total, neigh_total = lax.psum((self_part, neigh_part), ('rows', 'rep'))  239 us
    all_gather x1, waiting for transfers between devices, shards(): gathered = lax.all_gather(features, 'rows', axis=0, tiled=True)  116 us
    psum x1, waiting for transfers between devices, shards(): neighbour_sum = lax.psum(partial_rows, 'rep') * scale  23.8 us
  transfers between devices with their start and end apart: 4, of which 4 were waited for; matrix products, arithmetic and copies ran while one was open for 2% of the time, Pallas kernels for 0%

commit v1 on v0

v1 whole, which is shorter than its diff:
```python
import functools

import jax
import jax.numpy as jnp
from jax import lax
from jax.experimental import pallas as pl
from jax.experimental.pallas import tpu as pltpu
from jax.sharding import Mesh
from jax.sharding import PartitionSpec as P

edge_moment = 14.0 / 96.0
f32, bf16 = jnp.float32, jnp.bfloat16
CHUNK = 16
ALL = ("z", "y", "x", "rep")
VMEM_LIMIT = 40 * 2**20


def params():
    return pltpu.CompilerParams(vmem_limit_bytes=VMEM_LIMIT)


def whole(shape):
    return pl.BlockSpec(shape, lambda *_: (0,) * len(shape))


def spread(block, axes):
    count = 1
    for axis in axes:
        count *= lax.axis_size(axis)
    copies = jnp.broadcast_to(block[None], (count,) + block.shape)
    return lax.all_to_all(copies, axes, 0, 0, tiled=True)


def gather_kernel(place_ref, slot_ref, counts_ref, features_ref, out_ref):
    step = pl.program_id(0)

    @pl.when(step == 0)
    def _():
        out_ref[...] = jnp.zeros_like(out_ref)

    for k in range(CHUNK):
        tile = step * CHUNK + k
        counts = counts_ref[k].astype(f32).astype(bf16)
        product = jnp.dot(counts, features_ref[place_ref[tile]], preferred_element_type=f32)
        out_ref[slot_ref[tile]] += product


def gather_products(place, slot, tile_counts, gathered):
    tiles, block, _ = tile_counts.shape
    return pl.pallas_call(
        gather_kernel,
        out_shape=jax.ShapeDtypeStruct((2, block, gathered.shape[-1]), f32),
        grid_spec=pltpu.PrefetchScalarGridSpec(
            num_scalar_prefetch=2,
            grid=(tiles // CHUNK,),
            in_specs=[
                pl.BlockSpec((CHUNK, block, block), lambda i, *_: (i, 0, 0)),
                whole(gathered.shape),
            ],
            out_specs=whole((2, block, gathered.shape[-1])),
        ),
        compiler_params=params(),
        cost_estimate=pl.CostEstimate(
            flops=2 * tiles * block**3, bytes_accessed=tile_counts.size * 4 + gathered.size * 2, transcendentals=0
        ),
        name="gather_products",
    )(place, slot, tile_counts, gathered)


def dense_kernel(
    scale,
    own_ref,
    other_ref,
    feat_ref,
    feat_other_ref,
    masked_ref,
    masked_other_ref,
    self_ref,
    neigh_ref,
    act_ref,
    back_ref,
    term_ref,
    grad_ref,
):
    contract_last = (((1,), (1,)), ((), ()))
    contract_first = (((0,), (0,)), ((), ()))
    for s, (feat_in, masked_in) in enumerate(((feat_ref, masked_ref), (feat_other_ref, masked_other_ref))):
        feat = feat_in[...]
        neighbour = (scale * (own_ref[s] + other_ref[1 - s])).astype(bf16)
        preact = jnp.dot(feat, self_ref[...], preferred_element_type=f32) + jnp.dot(
            neighbour, neigh_ref[...], preferred_element_type=f32
        )
        sigma = jax.nn.sigmoid(preact)
        delta = (masked_in[...].astype(f32) * sigma * (1.0 + preact * (1.0 - sigma))).astype(bf16)
        back_ref[s] = lax.dot_general(
            neigh_ref[...], delta, contract_last, preferred_element_type=f32
        ).astype(bf16)
        if s == 0:
            act_ref[...] = (preact * sigma).astype(bf16)
            term_ref[...] = lax.dot_general(self_ref[...], delta, contract_last, preferred_element_type=f32)
            grad_ref[0] = lax.dot_general(feat, delta, contract_first, preferred_element_type=f32)
            grad_ref[1] = lax.dot_general(neighbour, delta, contract_first, preferred_element_type=f32)


def spread_kernel(place_ref, slot_ref, counts_ref, back_ref, out_ref):
    step = pl.program_id(0)

    @pl.when(step == 0)
    def _():
        out_ref[...] = jnp.zeros_like(out_ref)

    for k in range(CHUNK):
        tile = step * CHUNK + k
        counts = counts_ref[k].astype(f32).astype(bf16)
        term = jnp.dot(back_ref[slot_ref[tile]], counts, preferred_element_type=f32).astype(bf16)
        place = place_ref[tile]
        out_ref[place] = (out_ref[place].astype(f32) + term.astype(f32)).astype(bf16)


def spread_terms(place, slot, tile_counts, back):
    tiles, block, _ = tile_counts.shape
    places = lax.axis_size("z") * lax.axis_size("y") * lax.axis_size("x")
    width = back.shape[1]
    return pl.pallas_call(
        spread_kernel,
        out_shape=jax.ShapeDtypeStruct((places, width, block), bf16),
        grid_spec=pltpu.PrefetchScalarGridSpec(
            num_scalar_prefetch=2,
            grid=(tiles // CHUNK,),
            in_specs=[
                pl.BlockSpec((CHUNK, block, block), lambda i, *_: (i, 0, 0)),
                whole(back.shape),
            ],
            out_specs=whole((places, width, block)),
        ),
        compiler_params=params(),
        cost_estimate=pl.CostEstimate(
            flops=2 * tiles * block**3, bytes_accessed=tile_counts.size * 4 + places * width * block * 2, transcendentals=0
        ),
        name="spread_terms",
    )(place, slot, tile_counts, back)


def middle_kernel(in_ref, out_ref):
    total = in_ref[0, 0].astype(f32)
    for k in range(1, in_ref.shape[0]):
        total += in_ref[k, 0].astype(f32)
    out_ref[0] = total.astype(bf16)


def middle_sum(parts):
    sources, kept, rows, columns = parts.shape
    return pl.pallas_call(
        middle_kernel,
        out_shape=jax.ShapeDtypeStruct((kept, rows, columns), bf16),
        grid=(kept,),
        in_specs=[pl.BlockSpec((sources, 1, rows, columns), lambda i: (0, i, 0, 0))],
        out_specs=pl.BlockSpec((1, rows, columns), lambda i: (i, 0, 0)),
        compiler_params=params(),
        name="middle_sum",
    )(parts)


def last_kernel(scale, in_ref, term_ref, out_ref):
    total = in_ref[0].astype(f32)
    for k in range(1, in_ref.shape[0]):
        total += in_ref[k].astype(f32)
    out_ref[...] = (term_ref[...] + scale * total).T


def shards(
    features, tile_counts, tile_row, tile_col, label_ids, cotangent, self_weight, neigh_weight
):
    half_rows, width_in = features.shape
    hidden = cotangent.shape[1]
    tile_total, block, _ = tile_counts.shape
    planes, ys, xs, reps = (lax.axis_size(a) for a in ALL)
    rep = lax.axis_index("rep")
    scale = (edge_moment * tile_total * reps * block / 2) ** (-0.5)
    swap = [(0, 1), (1, 0)]

    owner = tile_col // reps
    place = (owner % (ys * xs)) * planes + owner // (ys * xs)
    slot = jnp.bitwise_xor(tile_row, rep)

    near = spread(features, ("z",))
    gathered = spread(near.reshape(planes, half_rows, width_in), ("y", "x"))
    gathered = gathered.reshape(-1, half_rows, width_in)

    local_ids = label_ids % half_rows
    label_mask = jnp.any(local_ids[:, None] == jnp.arange(half_rows, dtype=jnp.int32)[None, :], axis=0)
    masked = jnp.where(label_mask[:, None], cotangent, jnp.zeros_like(cotangent))
    features_other = lax.ppermute(features, "rep", swap)
    masked_other = lax.ppermute(masked, "rep", swap)

    own = gather_products(place, slot, tile_counts, gathered)
    other = lax.ppermute(own, "rep", swap)

    activation, back, own_term, grads = pl.pallas_call(
        functools.partial(dense_kernel, scale),
        out_shape=(
            jax.ShapeDtypeStruct((half_rows, hidden), bf16),
            jax.ShapeDtypeStruct((2, width_in, half_rows), bf16),
            jax.ShapeDtypeStruct((width_in, half_rows), f32),
            jax.ShapeDtypeStruct((2, width_in, hidden), f32),
        ),
        compiler_params=params(),
        name="dense",
    )(own, other, features, features_other, masked, masked_other, self_weight, neigh_weight)

    terms = spread_terms(place, slot, tile_counts, back)
    first = lax.all_to_all(
        terms.reshape(ys * xs, planes, width_in, block), ("y", "x"), 0, 0, tiled=True
    )
    second = lax.all_to_all(middle_sum(first), ("z",), 0, 0, tiled=True)
    grad_features = pl.pallas_call(
        functools.partial(last_kernel, scale),
        out_shape=jax.ShapeDtypeStruct((half_rows, width_in), f32),
        compiler_params=params(),
        name="last_sum",
    )(second, own_term)

    cells = grads.reshape(ys * xs, -1, 128)
    cells = jnp.sum(lax.all_to_all(cells, ("y", "x"), 0, 0, tiled=True), axis=0)
    cells = jnp.sum(spread(cells, ("z", "rep")), axis=0)
    totals = spread(cells, ("y", "x")).reshape(2, width_in, hidden)
    grad_scale = float(label_ids.shape[0] * planes * ys * xs * reps) ** (-0.5)
    totals = grad_scale * totals
    return activation, grad_features, totals[0], totals[1]


def solution(mesh):
    grid = Mesh(mesh.devices.reshape(8, 4, 4, 2), ALL)
    placed = (
        P(ALL, None),
        P(ALL, None, None),
        P(ALL),
        P(ALL),
        P(ALL),
        P(ALL, None),
        P(),
        P(),
    )
    return jax.shard_map(
        shards,
        mesh=grid,
        in_specs=placed,
        out_specs=(P(ALL, None), P(ALL, None), P(), P()),
        check_vma=False,
    )
```

time: 1180 us -> 233 us (0.20)
  the two profiles are of different devices: /device:TPU:0 before, /device:TPU:32 now
where the time goes in v1:
time: 233 us; the launch traced here: 232 us
  waiting for transfers between devices  133 us (57%)
  starting transfers between devices  34.5 us (15%)
  blocking collectives  31.5 us (14%)
  Pallas kernels  16.7 us (7%)
  local copies, waits for them, and re-layouts  15.4 us (7%)
    all_to_all x1, waiting for transfers between devices, shards(): lax.all_to_all(terms.reshape(ys * xs, planes, width_in, block), ('y', 'x'...  64.6 us
    all_to_all x3, waiting for transfers between devices, spread(): return lax.all_to_all(copies, axes, 0, 0, tiled=True)  58.3 us
    all_to_all x3, starting transfers between devices, spread(): return lax.all_to_all(copies, axes, 0, 0, tiled=True)  22.6 us
    all_to_all x1, blocking collectives, spread(): return lax.all_to_all(copies, axes, 0, 0, tiled=True)  18.8 us
    all_to_all x1, blocking collectives, shards(): cells = jnp.sum(lax.all_to_all(cells, ('y', 'x'), 0, 0, tiled=True), axis=0)  12.7 us
    unnamed x20, local copies, waits for them, and re-layouts  8.75 us
    all_to_all x1, waiting for transfers between devices, shards(): second = lax.all_to_all(middle_sum(first), ('z',), 0, 0, tiled=True)  8.7 us
    all_to_all x1, starting transfers between devices, shards(): second = lax.all_to_all(middle_sum(first), ('z',), 0, 0, tiled=True)  6.6 us
  transfers between devices with their start and end apart: 8, of which 6 were waited for; matrix products, arithmetic and copies ran while one was open for 1% of the time, Pallas kernels for 4%

profile of v1, /device:TPU:32, one launch (start us, length us, event | category | flops | bytes accessed | tf_op | source)
XLA Modules:
  0.0 231.9 jit_solution(5011787440746007917)
XLA Ops:
  0.6 0.8 broadcast_in_dim.18
  1.4 18.8 %all_to_all.35 = bf16[8,128,128]{2,1,0:T(8,128)(2,1)S(1)} all-to-all(bf16[8,128,128]{2,1,0:T(8,128)(2,1)S(1)} %broadcast_in_dim.18), channel_id=1, replica_groups=mesh['z'=8,'y'=4,'x'=4,'rep'=2] {'z'}, dimensions={0} | all-to-all | bytes 524288 | tf_op jit(solution)/shard_map/all_to_all | solution.py:31
  20.2 3.0 %broadcast_in_dim.19 = bf16[16,8,128,128]{3,2,1,0:T(8,128)(2,1)} broadcast(bf16[8,128,128]{2,1,0:T(8,128)(2,1)S(1)} %all_to_all.35), dimensions={1,2,3} | broadcast | bytes 4456448 | tf_op jit(solution)/shard_map/broadcast_in_dim | solution.py:30
  23.2 7.2 %all-to-all-start.1 = ((bf16[16,8,128,128]{3,2,1,0:T(8,128)(2,1)}), bf16[16,8,128,128]{3,2,1,0:T(8,128)(2,1)}, u32[]{:S(2)}, u32[]{:S(2)}) async-start(bf16[16,8,128,128]{3,2,1,0:T(8,128)(2,1)} %broadcast_in_dim.19), calls=%async_computation.1 | async-start | bytes 8388608 | tf_op jit(solution)/shard_map/all_to_all | solution.py:31
  30.6 55.2 %all-to-all-done.1 = bf16[16,8,128,128]{3,2,1,0:T(8,128)(2,1)} async-done(((bf16[16,8,128,128]{3,2,1,0:T(8,128)(2,1)}), bf16[16,8,128,128]{3,2,1,0:T(8,128)(2,1)}, u32[]{:S(2)}, u32[]{:S(2)}) %all-to-all-start.1) | async-done | bytes 4194336 | tf_op jit(solution)/shard_map/all_to_all | solution.py:31
  85.8 3.4 %copy-done = s32[128,128,128]{2,1,0:T(8,128)S(1)} copy-done((s32[128,128,128]{2,1,0:T(8,128)S(1)}, s32[128,128,128]{2,1,0:T(8,128)}, u32[]{:S(2)}) %copy-start) | copy-done | bytes 8388632
  89.2 5.3 %gather_products.1.own_ref = f32[2,128,128]{2,1,0:T(8,128)S(1)} custom-call(s32[128]{0:T(128)S(1)} %get-tuple-element.14.place_ref, s32[128]{0:T(128)S(1)} %get-tuple-element.15.slot_ref, s32[128,128,128]{2,1,0:T(8,128)S(1)} %copy-done, bf16[128,128,128]{2,1,0:T(8,128)(2,1)} %bitcast.features_ref), custom_call_target="tpu_custom_call" | custom-call | flops 536870912 | bytes 12582912 | tf_op jit(solution)/shard_map/gather_products/pallas_call | solution.py:50
  95.4 1.1 collective-permute-done.1.feat_other_ref
  96.5 0.8 dense.1
  97.4 12.7 %all_to_all.36 = f32[16,32,128]{2,1,0:T(8,128)S(1)} all-to-all(f32[16,32,128]{2,1,0:T(8,128)S(1)} %reshape.32), channel_id=1, replica_groups=mesh['z'=8,'y'=4,'x'=4,'rep'=2] {'y','x'}, dimensions={0} | all-to-all | bytes 524288 | tf_op jit(solution)/shard_map/all_to_all | solution.py:224
  110.1 0.7 broadcast_in_dim.22
  110.8 10.6 %all-to-all-start.5 = ((f32[16,32,128]{2,1,0:T(8,128)}), f32[16,32,128]{2,1,0:T(8,128)S(1)}, u32[]{:S(2)}, u32[]{:S(2)}) async-start(f32[16,32,128]{2,1,0:T(8,128)} %broadcast_in_dim.22), calls=%async_computation.5 | async-start | bytes 524288 | tf_op jit(solution)/shard_map/all_to_all | solution.py:31
  121.4 3.4 %copy-done.1 = s32[128,128,128]{2,1,0:T(8,128)S(1)} copy-done((s32[128,128,128]{2,1,0:T(8,128)S(1)}, s32[128,128,128]{2,1,0:T(8,128)}, u32[]{:S(2)}) %copy-start.1) | copy-done | bytes 8388632
  124.8 3.9 %spread_terms.1 = bf16[128,128,128]{2,1,0:T(8,128)(2,1)S(1)} custom-call(s32[128]{0:T(128)S(1)} %get-tuple-element.14.place_ref, s32[128]{0:T(128)S(1)} %get-tuple-element.15.slot_ref, s32[128,128,128]{2,1,0:T(8,128)S(1)} %copy-done.1, bf16[2,128,128]{2,1,0:T(8,128)(2,1)S(1)} %get-tuple-element.9.back_ref), custom_call_target="tpu_custom_call" | custom-call | flops 536870912 | bytes 12582912 | tf_op jit(solution)/shard_map/spread_terms/pallas_call | solution.py:124
  128.8 2.0 copy-done.2
  131.1 4.5 %all-to-all-start.2 = ((bf16[16,8,128,128]{3,2,1,0:T(8,128)(2,1)}), bf16[16,8,128,128]{3,2,1,0:T(8,128)(2,1)}, u32[]{:S(2)}, u32[]{:S(2)}) async-start(bf16[16,8,128,128]{3,2,1,0:T(8,128)(2,1)} %bitcast.2), calls=%async_computation.2 | async-start | bytes 8388608 | tf_op jit(solution)/shard_map/all_to_all | solution.py:212
  135.6 64.6 %all-to-all-done.2.in_ref = bf16[16,8,128,128]{3,2,1,0:T(8,128)(2,1)} async-done(((bf16[16,8,128,128]{3,2,1,0:T(8,128)(2,1)}), bf16[16,8,128,128]{3,2,1,0:T(8,128)(2,1)}, u32[]{:S(2)}, u32[]{:S(2)}) %all-to-all-start.2) | async-done | bytes 4194336 | tf_op jit(solution)/shard_map/all_to_all | solution.py:212
  200.2 0.7 broadcast_in_dim.23
  201.0 4.8 %all-to-all-start.6 = ((f32[16,32,128]{2,1,0:T(8,128)}), f32[16,32,128]{2,1,0:T(8,128)S(1)}, u32[]{:S(2)}, u32[]{:S(2)}) async-start(f32[16,32,128]{2,1,0:T(8,128)} %broadcast_in_dim.23), calls=%async_computation.6 | async-start | bytes 524288 | tf_op jit(solution)/shard_map/all_to_all | solution.py:31
  205.7 5.8 %middle_sum.1 = bf16[8,128,128]{2,1,0:T(8,128)(2,1)} custom-call(bf16[16,8,128,128]{3,2,1,0:T(8,128)(2,1)} %all-to-all-done.2.in_ref), custom_call_target="tpu_custom_call" | custom-call | tf_op jit(solution)/shard_map/middle_sum/pallas_call | solution.py:153
  211.6 2.9 %all-to-all-done.6 = f32[16,32,128]{2,1,0:T(8,128)S(1)} async-done(((f32[16,32,128]{2,1,0:T(8,128)}), f32[16,32,128]{2,1,0:T(8,128)S(1)}, u32[]{:S(2)}, u32[]{:S(2)}) %all-to-all-start.6) | async-done | bytes 262176 | tf_op jit(solution)/shard_map/all_to_all | solution.py:31
  214.4 6.6 %all-to-all-start.3 = ((bf16[8,128,128]{2,1,0:T(8,128)(2,1)}), bf16[8,128,128]{2,1,0:T(8,128)(2,1)S(1)}, u32[]{:S(2)}, u32[]{:S(2)}) async-start(bf16[8,128,128]{2,1,0:T(8,128)(2,1)} %middle_sum.1), calls=%async_computation.3 | async-start | bytes 524288 | tf_op jit(solution)/shard_map/all_to_all | solution.py:215
  222.5 8.7 %all-to-all-done.3.in_ref = bf16[8,128,128]{2,1,0:T(8,128)(2,1)S(1)} async-done(((bf16[8,128,128]{2,1,0:T(8,128)(2,1)}), bf16[8,128,128]{2,1,0:T(8,128)(2,1)S(1)}, u32[]{:S(2)}, u32[]{:S(2)}) %all-to-all-start.3) | async-done | bytes 262176 | tf_op jit(solution)/shard_map/all_to_all | solution.py:215
  231.2 0.7 last_sum.1
  (34 shorter events, 2.8 us)
Async XLA Ops:
  23.2 7.2 %copy-start.9 = (s32[64]{0:T(128)S(1)}, s32[64]{0:T(128)}, u32[]{:S(2)}) copy-start(s32[64]{0:T(128)} %param.12) | copy-start | bytes 772
  23.2 7.4 %copy-start.7 = (s32[128]{0:T(128)S(1)}, s32[128]{0:T(128)}, u32[]{:S(2)}) copy-start(s32[128]{0:T(128)} %param.11) | copy-start | bytes 1540
  23.2 7.4 %copy-start.8 = (s32[128]{0:T(128)S(1)}, s32[128]{0:T(128)}, u32[]{:S(2)}) copy-start(s32[128]{0:T(128)} %param.10) | copy-start | bytes 1540
  23.2 62.5 %all-to-all-start.1 = ((bf16[16,8,128,128]{3,2,1,0:T(8,128)(2,1)}), bf16[16,8,128,128]{3,2,1,0:T(8,128)(2,1)}, u32[]{:S(2)}, u32[]{:S(2)}) async-start(bf16[16,8,128,128]{3,2,1,0:T(8,128)(2,1)} %broadcast_in_dim.19), calls=%async_computation.1 | async-start | bytes 8388608 | tf_op jit(solution)/shard_map/all_to_all | solution.py:31
  85.8 3.4 %copy-start = (s32[128,128,128]{2,1,0:T(8,128)S(1)}, s32[128,128,128]{2,1,0:T(8,128)}, u32[]{:S(2)}) copy-start(s32[128,128,128]{2,1,0:T(8,128)} %counts_ref.3) | copy-start | bytes 25165828
  89.2 5.4 %copy-start.6 = (bf16[128,256]{1,0:T(8,128)(2,1)S(1)}, bf16[128,256]{1,0:T(8,128)(2,1)}, u32[]{:S(2)}) copy-start(bf16[128,256]{1,0:T(8,128)(2,1)} %param.13) | copy-start | bytes 196612
  89.2 6.1 %copy-start.3 = (bf16[128,128]{1,0:T(8,128)(2,1)S(1)}, bf16[128,128]{1,0:T(8,128)(2,1)}, u32[]{:S(2)}) copy-start(bf16[128,128]{1,0:T(8,128)(2,1)} %feat_ref.1) | copy-start | bytes 98308
  89.2 7.3 %copy-start.4 = (bf16[128,256]{1,0:T(8,128)(2,1)S(1)}, bf16[128,256]{1,0:T(8,128)(2,1)}, u32[]{:S(2)}) copy-start(bf16[128,256]{1,0:T(8,128)(2,1)} %self_ref.1) | copy-start | bytes 196612
  89.2 7.3 %copy-start.5 = (bf16[128,256]{1,0:T(8,128)(2,1)S(1)}, bf16[128,256]{1,0:T(8,128)(2,1)}, u32[]{:S(2)}) copy-start(bf16[128,256]{1,0:T(8,128)(2,1)} %neigh_ref.1) | copy-start | bytes 196612
  94.5 2.0 collective-permute-start
  94.7 1.8 collective-permute-start.2
  95.3 1.2 collective-permute-start.1
  110.8 20.2 %all-to-all-start.5 = ((f32[16,32,128]{2,1,0:T(8,128)}), f32[16,32,128]{2,1,0:T(8,128)S(1)}, u32[]{:S(2)}, u32[]{:S(2)}) async-start(f32[16,32,128]{2,1,0:T(8,128)} %broadcast_in_dim.22), calls=%async_computation.5 | async-start | bytes 524288 | tf_op jit(solution)/shard_map/all_to_all | solution.py:31
  121.4 3.4 %copy-start.1 = (s32[128,128,128]{2,1,0:T(8,128)S(1)}, s32[128,128,128]{2,1,0:T(8,128)}, u32[]{:S(2)}) copy-start(s32[128,128,128]{2,1,0:T(8,128)} %counts_ref.3) | copy-start | bytes 25165828
  128.8 2.0 copy-start.2
  131.1 69.2 %all-to-all-start.2 = ((bf16[16,8,128,128]{3,2,1,0:T(8,128)(2,1)}), bf16[16,8,128,128]{3,2,1,0:T(8,128)(2,1)}, u32[]{:S(2)}, u32[]{:S(2)}) async-start(bf16[16,8,128,128]{3,2,1,0:T(8,128)(2,1)} %bitcast.2), calls=%async_computation.2 | async-start | bytes 8388608 | tf_op jit(solution)/shard_map/all_to_all | solution.py:212
  201.0 13.5 %all-to-all-start.6 = ((f32[16,32,128]{2,1,0:T(8,128)}), f32[16,32,128]{2,1,0:T(8,128)S(1)}, u32[]{:S(2)}, u32[]{:S(2)}) async-start(f32[16,32,128]{2,1,0:T(8,128)} %broadcast_in_dim.23), calls=%async_computation.6 | async-start | bytes 524288 | tf_op jit(solution)/shard_map/all_to_all | solution.py:31
  214.4 16.7 %all-to-all-start.3 = ((bf16[8,128,128]{2,1,0:T(8,128)(2,1)}), bf16[8,128,128]{2,1,0:T(8,128)(2,1)S(1)}, u32[]{:S(2)}, u32[]{:S(2)}) async-start(bf16[8,128,128]{2,1,0:T(8,128)(2,1)} %middle_sum.1), calls=%async_computation.3 | async-start | bytes 524288 | tf_op jit(solution)/shard_map/all_to_all | solution.py:215

commit v2 on v1

v2 whole, which is shorter than its diff:
```python
import functools

import jax
import jax.numpy as jnp
from jax import lax
from jax.experimental import pallas as pl
from jax.experimental.pallas import tpu as pltpu
from jax.sharding import Mesh
from jax.sharding import PartitionSpec as P

edge_moment = 14.0 / 96.0
f32, bf16 = jnp.float32, jnp.bfloat16
CHUNK = 16
HIGH, LOW = ("zq", "yq", "xq"), ("zp", "yp", "xp", "rep")
ROWS = ("zq", "zp", "yq", "yp", "xq", "xp")
ALL = ROWS + ("rep",)
VMEM_LIMIT = 24 * 2**20
SMEM = pl.BlockSpec(memory_space=pltpu.SMEM)
VMEM = pl.BlockSpec(memory_space=pltpu.VMEM)
def params():
    return pltpu.CompilerParams(vmem_limit_bytes=VMEM_LIMIT)


def whole(shape):
    return pl.BlockSpec(shape, lambda *_: (0,) * len(shape))


def move(block, dz, dy, dx):
    pairs = [
        (z * 16 + y * 4 + x, (z + dz) % 8 * 16 + (y + dy) % 4 * 4 + (x + dx) % 4)
        for z in range(8)
        for y in range(4)
        for x in range(4)
    ]
    return lax.ppermute(block, ROWS, pairs)


def spread(block, axes):
    count = 1
    for axis in axes:
        count *= lax.axis_size(axis)
    copies = jnp.broadcast_to(block[None], (count,) + block.shape)
    return lax.all_to_all(copies, axes, 0, 0, tiled=True)


DETOUR = ((0, 0, 0), (0, 0, -1), (0, -1, 0), (2, 1, 1), (-1, 0, 0), (1, 2, 1), (1, 1, 2), (1, 1, 1))


def place_of(near, far):
    parity = jnp.bitwise_xor(near, far)
    parity = (parity >> 4 & 1) * 4 + (parity >> 2 & 1) * 2 + (parity & 1)
    extra = [sum(jnp.where(parity == c, step[k], 0) for c, step in enumerate(DETOUR)) for k in range(3)]
    z = ((far >> 4) - (near >> 4) + extra[0]) & 7
    y = ((far >> 2 & 3) - (near >> 2 & 3) + extra[1]) & 3
    x = ((far & 3) - (near & 3) + extra[2]) & 3
    return (parity * 16 + (y >> 1) * 8 + (x >> 1) * 4 + (z >> 1)).astype(jnp.int32)


def cast_kernel(in_ref, out_ref):
    out_ref[...] = in_ref[...].astype(f32).astype(bf16)


def cast_counts(tile_counts):
    tiles, block, _ = tile_counts.shape
    spec = pl.BlockSpec((CHUNK, block, block), lambda i: (i, 0, 0))
    return pl.pallas_call(
        cast_kernel,
        out_shape=jax.ShapeDtypeStruct(tile_counts.shape, bf16),
        grid=(tiles // CHUNK,),
        in_specs=[spec],
        out_specs=spec,
        compiler_params=params(),
        cost_estimate=pl.CostEstimate(flops=tile_counts.size, bytes_accessed=tile_counts.size * 6, transcendentals=0),
        name="cast_counts",
    )(tile_counts)


def gather_kernel(place_ref, slot_ref, counts_ref, *refs):
    parts, (out_ref, held_ref) = refs[:8], refs[8:]
    for k, part in enumerate(parts):
        held_ref[16 * k : 16 * k + 16] = part[...]
    out_ref[...] = jnp.zeros_like(out_ref)

    @pl.loop(0, counts_ref.shape[0] // CHUNK)
    def _(step):
        for k in range(CHUNK):
            tile = step * CHUNK + k
            product = jnp.dot(counts_ref[tile], held_ref[place_ref[tile]], preferred_element_type=f32)
            out_ref[slot_ref[tile]] += product


def gather_products(place, slot, counts, parts):
    tiles, block, _ = counts.shape
    width = parts[0].shape[-1]
    return pl.pallas_call(
        gather_kernel,
        out_shape=jax.ShapeDtypeStruct((2, block, width), f32),
        in_specs=[SMEM] * 2 + [VMEM] * 9,
        out_specs=VMEM,
        scratch_shapes=[pltpu.VMEM((128, block, width), bf16)],
        compiler_params=params(),
        cost_estimate=pl.CostEstimate(flops=2 * tiles * block**3, bytes_accessed=counts.size * 4, transcendentals=0),
        name="gather_products",
    )(place, slot, counts, *parts)


def dense_kernel(
    scale,
    own_ref,
    other_ref,
    feat_ref,
    feat_other_ref,
    masked_ref,
    masked_other_ref,
    self_ref,
    neigh_ref,
    act_ref,
    back_ref,
    term_ref,
    grad_ref,
):
    contract_last = (((1,), (1,)), ((), ()))
    contract_first = (((0,), (0,)), ((), ()))
    for s, (feat_in, masked_in) in enumerate(((feat_ref, masked_ref), (feat_other_ref, masked_other_ref))):
        feat = feat_in[...]
        neighbour = (scale * (own_ref[s] + other_ref[1 - s])).astype(bf16)
        preact = jnp.dot(feat, self_ref[...], preferred_element_type=f32) + jnp.dot(
            neighbour, neigh_ref[...], preferred_element_type=f32
        )
        sigma = jax.nn.sigmoid(preact)
        delta = (masked_in[...].astype(f32) * sigma * (1.0 + preact * (1.0 - sigma))).astype(bf16)
        back_ref[s] = lax.dot_general(
            neigh_ref[...], delta, contract_last, preferred_element_type=f32
        ).astype(bf16)
        if s == 0:
            act_ref[...] = (preact * sigma).astype(bf16)
            term_ref[...] = lax.dot_general(self_ref[...], delta, contract_last, preferred_element_type=f32)
            for k, value in enumerate((feat, neighbour)):
                grad = lax.dot_general(value, delta, contract_first, preferred_element_type=f32)
                grad_ref[2 * k], grad_ref[2 * k + 1] = grad[:, :128], grad[:, 128:]


def spread_kernel(place_ref, slot_ref, counts_ref, back_ref, *refs):
    outs, held_ref = refs[:8], refs[8]
    held_ref[...] = jnp.zeros_like(held_ref)

    @pl.loop(0, counts_ref.shape[0] // CHUNK)
    def _(step):
        for k in range(CHUNK):
            tile = step * CHUNK + k
            term = jnp.dot(back_ref[slot_ref[tile]], counts_ref[tile], preferred_element_type=f32).astype(bf16)
            place = place_ref[tile]
            held_ref[place] = (held_ref[place].astype(f32) + term.astype(f32)).astype(bf16)

    for k, out in enumerate(outs):
        out[...] = held_ref[16 * k : 16 * k + 16]


def spread_terms(place, slot, counts, back):
    tiles, block, _ = counts.shape
    width = back.shape[1]
    return pl.pallas_call(
        spread_kernel,
        out_shape=[jax.ShapeDtypeStruct((16, width, block), bf16)] * 8,
        in_specs=[SMEM] * 2 + [VMEM] * 2,
        out_specs=[VMEM] * 8,
        scratch_shapes=[pltpu.VMEM((128, width, block), bf16)],
        compiler_params=params(),
        cost_estimate=pl.CostEstimate(flops=2 * tiles * block**3, bytes_accessed=counts.size * 4, transcendentals=0),
        name="spread_terms",
    )(place, slot, counts, back)


def add_up(refs, index):
    total = refs[0][index].astype(f32)
    for ref in refs[1:]:
        total += ref[index].astype(f32)
    return total


def class_kernel(*refs):
    @pl.loop(0, refs[0].shape[0])
    def _(k):
        refs[-1][k] = add_up(refs[:-1], k).astype(bf16)


def class_sum(parts):
    return pl.pallas_call(
        class_kernel,
        out_shape=jax.ShapeDtypeStruct(parts[0].shape, bf16),
        in_specs=[VMEM] * len(parts),
        out_specs=VMEM,
        compiler_params=params(),
        name="class_sum",
    )(*parts)


def joint_kernel(cells_ref, *refs):
    ins, outs = refs[:5], refs[5:]
    rows = ins[0].shape[1]
    for k, out in enumerate(outs):
        for z in range(4):
            out[z * rows : z * rows + rows] = add_up(ins, 4 * k + z).astype(bf16)
        out[4 * rows :] = cells_ref[...].astype(bf16)


def joint_sum(cells, parts):
    _, rows, columns = parts[0].shape
    return pl.pallas_call(
        joint_kernel,
        out_shape=[jax.ShapeDtypeStruct((4 * rows + cells.shape[0], columns), bf16)] * 4,
        in_specs=[VMEM] * 6,
        out_specs=[VMEM] * 4,
        compiler_params=params(),
        name="joint_sum",
    )(cells, *parts)


def plane_kernel(*refs):
    ins, outs = refs[:4], refs[4:]
    rows = 128
    for z, out in enumerate(outs):
        out[:rows] = add_up(ins, slice(z * rows, z * rows + rows)).astype(bf16)
        for k, part in enumerate(ins):
            out[rows + 32 * k : rows + 32 * k + 32] = part[4 * rows :]


def plane_sum(parts):
    columns = parts[0].shape[1]
    return pl.pallas_call(
        plane_kernel,
        out_shape=[jax.ShapeDtypeStruct((256, columns), bf16)] * 4,
        in_specs=[VMEM] * 4,
        out_specs=[VMEM] * 4,
        compiler_params=params(),
        name="plane_sum",
    )(*parts)


def last_kernel(scale, grad_scale, order_ref, *refs):
    ins, (term_ref, out_ref, self_ref, neigh_ref, cells_ref) = refs[:4], refs[4:]
    rows = term_ref.shape[0]
    total = add_up(ins, slice(0, rows))
    out_ref[...] = (term_ref[...] + scale * total).T
    for z, part in enumerate(ins):
        for k in range(4):
            cells = part[rows + 32 * k : rows + 32 * k + 32].astype(f32)
            cells_ref[order_ref[4 * k + z]] = grad_scale * cells
    for k in range(16):
        ref = (self_ref, neigh_ref)[k // 8]
        ref[k % 4 * 32 : k % 4 * 32 + 32, k // 4 % 2 * 128 : k // 4 % 2 * 128 + 128] = cells_ref[k]


def gather_blocks(features, tile_counts):
    own = features[None]
    own = jnp.concatenate([own, move(own, 2, 0, 0), move(own, 4, 0, 0), move(own, -2, 0, 0)])
    own = jnp.concatenate([own, move(own, 0, 0, 2), move(own, 0, 2, 0), move(own, 0, 2, 2)])
    own, tile_counts = lax.optimization_barrier((own, tile_counts))
    far = move(own, -1, -1, -1)
    by_x, by_y, by_z = move(own, 0, 0, 1), move(own, 0, 1, 0), move(own, 1, 0, 0)
    parts = [own, by_x, by_y, move(far, -1, 0, 0), by_z, move(far, 0, -1, 0), move(far, 0, 0, -1), far]
    return parts, tile_counts


def reduce_blocks(terms):
    far = class_sum([terms[7], move(terms[6], 0, 0, -1), move(terms[5], 0, -1, 0), move(terms[3], -1, 0, 0)])
    direct = [move(terms[1], 0, 0, 1), move(terms[2], 0, 1, 0), move(terms[4], 1, 0, 0)]
    return [terms[0], *direct, move(far, -1, -1, -1)]


def shards(
    features, tile_counts, tile_row, tile_col, label_ids, cotangent, self_weight, neigh_weight
):
    half_rows, width_in = features.shape
    hidden = cotangent.shape[1]
    tile_total, block, _ = tile_counts.shape
    reps, devices = lax.axis_size("rep"), lax.axis_size(ALL)
    rep = lax.axis_index("rep")
    scale = (edge_moment * tile_total * reps * block / 2) ** (-0.5)
    swap = [(0, 1), (1, 0)]

    owner, here = tile_col // reps, lax.axis_index(ROWS)
    source, target = place_of(owner, here), place_of(here, owner)
    step = jnp.arange(16, dtype=jnp.int32)
    order = (here // 32 - step % 4) % 4 * 4 + (here // 8 + step // 8) % 2 * 2 + (here // 2 + step // 4) % 2
    slot = jnp.bitwise_xor(tile_row, rep)

    gathered, tile_counts = gather_blocks(features, tile_counts)
    counts = cast_counts(tile_counts)

    local_ids = label_ids % half_rows
    label_mask = jnp.any(local_ids[:, None] == jnp.arange(half_rows, dtype=jnp.int32)[None, :], axis=0)
    masked = jnp.where(label_mask[:, None], cotangent, jnp.zeros_like(cotangent))
    features_other = lax.ppermute(features, "rep", swap)
    masked_other = lax.ppermute(masked, "rep", swap)

    own = gather_products(source, slot, counts, gathered)
    other = lax.ppermute(own, "rep", swap)

    activation, back, own_term, grads = pl.pallas_call(
        functools.partial(dense_kernel, scale),
        out_shape=(
            jax.ShapeDtypeStruct((half_rows, hidden), bf16),
            jax.ShapeDtypeStruct((2, width_in, half_rows), bf16),
            jax.ShapeDtypeStruct((width_in, half_rows), f32),
            jax.ShapeDtypeStruct((4, width_in, 128), f32),
        ),
        compiler_params=params(),
        name="dense",
    )(own, other, features, features_other, masked, masked_other, self_weight, neigh_weight)

    terms = spread_terms(target, slot, counts, back)
    *terms, grads = lax.optimization_barrier((*terms, grads))
    parts = reduce_blocks(terms)

    cells = grads.reshape(lax.axis_size(HIGH), -1, 128)
    cells = jnp.sum(lax.all_to_all(cells, HIGH, 0, 0, tiled=True), axis=0)
    cells = jnp.sum(spread(cells, LOW), axis=0)
    parts = joint_sum(cells, parts)
    parts = plane_sum([parts[0], move(parts[1], 0, 0, 2), move(parts[2], 0, 2, 0), move(parts[3], 0, 2, 2)])
    parts = [parts[0], move(parts[1], 2, 0, 0), move(parts[2], 4, 0, 0), move(parts[3], -2, 0, 0)]
    grad_scale = float(label_ids.shape[0] * devices) ** (-0.5)
    grad_shape = jax.ShapeDtypeStruct((width_in, hidden), f32)
    grad_features, grad_self, grad_neigh = pl.pallas_call(
        functools.partial(last_kernel, scale, grad_scale),
        out_shape=(jax.ShapeDtypeStruct((half_rows, width_in), f32), grad_shape, grad_shape),
        in_specs=[SMEM] + [VMEM] * 5,
        out_specs=(VMEM, VMEM, VMEM),
        scratch_shapes=[pltpu.VMEM((16, 32, 128), f32)],
        compiler_params=params(),
        name="last_sum",
    )(order, *parts, own_term)
    return activation, grad_features, grad_self, grad_neigh


def solution(mesh):
    grid = Mesh(mesh.devices.reshape(4, 2, 2, 2, 2, 2, 2), ALL)
    placed = (
        P(ALL, None),
        P(ALL, None, None),
        P(ALL),
        P(ALL),
        P(ALL),
        P(ALL, None),
        P(),
        P(),
    )
    return jax.shard_map(
        shards,
        mesh=grid,
        in_specs=placed,
        out_specs=(P(ALL, None), P(ALL, None), P(), P()),
        check_vma=False,
    )
```

time: 233 us -> 146 us (0.63)
  waiting for transfers between devices: 133 us -> 46.7 us
  starting transfers between devices: 34.5 us -> 62.7 us
  blocking collectives: 31.5 us -> 12.1 us
  local copies, waits for them, and re-layouts: 15.4 us -> 5.07 us
  other arithmetic: 0.27 us -> 3.99 us
  Pallas kernels: 16.7 us -> 14.3 us
    all_to_all x5 -> x1, waiting for transfers between devices: 132 us -> 0.03 us  [shards(): cells = jnp.sum(lax.all_to_all(cells, HIGH, 0, 0, tiled=True), axis=0)]
    ppermute x0 -> x26, starting transfers between devices: none -> 54.5 us  [move(): return lax.ppermute(block, ROWS, pairs)]
    ppermute x0 -> x26, waiting for transfers between devices: none -> 45.7 us  [move(): return lax.ppermute(block, ROWS, pairs)]
    all_to_all x5 -> x1, starting transfers between devices: 33.7 us -> 7.25 us  [shards(): cells = jnp.sum(lax.all_to_all(cells, HIGH, 0, 0, tiled=True), axis=0)]
    all_to_all x1 -> x0, blocking collectives: 12.7 us -> none  [shards(): cells = jnp.sum(lax.all_to_all(cells, ('y', 'x'), 0, 0, tiled=True), axis=0)]
    all_to_all x1, blocking collectives: 18.8 us -> 12.1 us  [spread(): return lax.all_to_all(copies, axes, 0, 0, tiled=True)]
    broadcast_in_dim x4 -> x1, local copies, waits for them, and re-layouts: 5.26 us -> 0.02 us  [spread(): copies = jnp.broadcast_to(block[None], (count,) + block.shape)]
    unnamed x20 -> x18, local copies, waits for them, and re-layouts: 8.75 us -> 5.04 us
  transfers between devices with their start and end apart: 8 -> 30, of which waited for: 6 -> 14; matrix products, arithmetic and copies ran while one was open for 1% -> 3% of each run, Pallas kernels for 4% -> 2%
where the time goes in v2:
time: 146 us
  starting transfers between devices  62.7 us (43%)
  waiting for transfers between devices  46.7 us (32%)
  Pallas kernels  14.3 us (10%)
  blocking collectives  12.1 us (8%)
  local copies, waits for them, and re-layouts  5.07 us (3%)
  other arithmetic  3.99 us (3%)
    ppermute x26, starting transfers between devices, move(): return lax.ppermute(block, ROWS, pairs)  54.5 us
    ppermute x26, waiting for transfers between devices, move(): return lax.ppermute(block, ROWS, pairs)  45.7 us
    all_to_all x1, blocking collectives, spread(): return lax.all_to_all(copies, axes, 0, 0, tiled=True)  12.1 us
    all_to_all x1, starting transfers between devices, shards(): cells = jnp.sum(lax.all_to_all(cells, HIGH, 0, 0, tiled=True), axis=0)  7.25 us
    pallas_call x1, Pallas kernels, spread_terms(): pl.pallas_call(spread_kernel, out_shape=[jax.ShapeDtypeStruct((16, width,...  5.19 us
    unnamed x18, local copies, waits for them, and re-layouts  5.04 us
    pallas_call x1, Pallas kernels, gather_products(): pl.pallas_call(gather_kernel, out_shape=jax.ShapeDtypeStruct((2, block, w...  3.4 us
  transfers between devices with their start and end apart: 30, of which 14 were waited for; matrix products, arithmetic and copies ran while one was open for 3% of the time, Pallas kernels for 2%

profile of v2, /device:TPU:32, one launch (start us, length us, event | category | flops | bytes accessed | tf_op | source)
XLA Modules:
  0.0 145.7 jit_solution(4782602694706159715)
XLA Ops:
  0.6 5.5 %collective-permute-start.2 = (bf16[1,128,128]{2,1,0:T(8,128)(2,1)}, bf16[1,128,128]{2,1,0:T(8,128)(2,1)S(1)}, u32[]{:S(2)}, u32[]{:S(2)}) collective-permute-start(bf16[1,128,128]{2,1,0:T(8,128)(2,1)} %bitcast.3), channel_id=1, source_target_pairs={{0,192},{2,194},{4,196},{6,198},{8,200},{10,202},{12,204},{14,206}... | collective-permute-start | bytes 98312 | tf_op jit(solution)/shard_map/ppermute | solution.py:35
  7.5 2.4 %collective-permute-start = (bf16[1,128,128]{2,1,0:T(8,128)(2,1)}, bf16[1,128,128]{2,1,0:T(8,128)(2,1)S(1)}, u32[]{:S(2)}, u32[]{:S(2)}) collective-permute-start(bf16[1,128,128]{2,1,0:T(8,128)(2,1)} %bitcast.5), channel_id=1, source_target_pairs={{0,64},{2,66},{4,68},{6,70},{8,72},{10,74},{12,76},{14,78},{16,80}... | collective-permute-start | bytes 98312 | tf_op jit(solution)/shard_map/ppermute | solution.py:35
  10.7 3.4 %collective-permute-done.1 = bf16[1,128,128]{2,1,0:T(8,128)(2,1)S(1)} collective-permute-done((bf16[1,128,128]{2,1,0:T(8,128)(2,1)}, bf16[1,128,128]{2,1,0:T(8,128)(2,1)S(1)}, u32[]{:S(2)}, u32[]{:S(2)}) %collective-permute-start.1) | collective-permute-done | bytes 32800 | tf_op jit(solution)/shard_map/ppermute | solution.py:35
  14.9 5.7 %collective-permute-start.5 = (bf16[4,128,128]{2,1,0:T(8,128)(2,1)S(1)}, bf16[4,128,128]{2,1,0:T(8,128)(2,1)S(1)}, u32[]{:S(2)}, u32[]{:S(2)}) collective-permute-start(bf16[4,128,128]{2,1,0:T(8,128)(2,1)S(1)} %pad_maximum_fusion), channel_id=1, source_target_pairs={{0,20},{2,22},{4,16},{6,18},{8,28},{10,30},{12,24},{14,26},{16,4},... | collective-permute-start | bytes 393224 | tf_op jit(solution)/shard_map/ppermute | solution.py:35
  21.5 5.9 %collective-permute-done.3 = bf16[4,128,128]{2,1,0:T(8,128)(2,1)S(1)} collective-permute-done((bf16[4,128,128]{2,1,0:T(8,128)(2,1)S(1)}, bf16[4,128,128]{2,1,0:T(8,128)(2,1)S(1)}, u32[]{:S(2)}, u32[]{:S(2)}) %collective-permute-start.3) | collective-permute-done | bytes 131104 | tf_op jit(solution)/shard_map/ppermute | solution.py:35
  27.6 4.2 %collective-permute-start.8 = (bf16[16,128,128]{2,1,0:T(8,128)(2,1)S(1)}, bf16[16,128,128]{2,1,0:T(8,128)(2,1)S(1)}, u32[]{:S(2)}, u32[]{:S(2)}) collective-permute-start(bf16[16,128,128]{2,1,0:T(8,128)(2,1)S(1)} %constant_dynamic-update-slice_fusion.refs_0_), channel_id=1, source_target_pairs={{0,254},{2,248},{4,250},{6,252},{8,230},{10,224},{12,226},{14,228}... | collective-permute-start | bytes 1572872 | tf_op jit(solution)/shard_map/ppermute | solution.py:35
  34.3 6.8 %collective-permute-done.8.refs_7_ = bf16[16,128,128]{2,1,0:T(8,128)(2,1)S(1)} collective-permute-done((bf16[16,128,128]{2,1,0:T(8,128)(2,1)S(1)}, bf16[16,128,128]{2,1,0:T(8,128)(2,1)S(1)}, u32[]{:S(2)}, u32[]{:S(2)}) %collective-permute-start.8) | collective-permute-done | bytes 524320 | tf_op jit(solution)/shard_map/ppermute | solution.py:35
  41.1 2.6 %collective-permute-start.12 = (bf16[16,128,128]{2,1,0:T(8,128)(2,1)S(1)}, bf16[16,128,128]{2,1,0:T(8,128)(2,1)S(1)}, u32[]{:S(2)}, u32[]{:S(2)}) collective-permute-start(bf16[16,128,128]{2,1,0:T(8,128)(2,1)S(1)} %collective-permute-done.8.refs_7_), channel_id=1, source_target_pairs={{0,6},{2,0},{4,2},{6,4},{8,14},{10,8},{12,10},{14,12},{16,22},{18,... | collective-permute-start | bytes 1572872 | tf_op jit(solution)/shard_map/ppermute | solution.py:35
  43.8 3.9 %collective-permute-start.11 = (bf16[16,128,128]{2,1,0:T(8,128)(2,1)S(1)}, bf16[16,128,128]{2,1,0:T(8,128)(2,1)S(1)}, u32[]{:S(2)}, u32[]{:S(2)}) collective-permute-start(bf16[16,128,128]{2,1,0:T(8,128)(2,1)S(1)} %collective-permute-done.8.refs_7_), channel_id=1, source_target_pairs={{0,24},{2,26},{4,28},{6,30},{8,0},{10,2},{12,4},{14,6},{16,8},{18,... | collective-permute-start | bytes 1572872 | tf_op jit(solution)/shard_map/ppermute | solution.py:35
  50.3 3.4 %copy-done = s32[128,128,128]{2,1,0:T(8,128)S(1)} copy-done((s32[128,128,128]{2,1,0:T(8,128)S(1)}, s32[128,128,128]{2,1,0:T(8,128)}, u32[]{:S(2)}) %copy-start) | copy-done | bytes 8388632
  54.3 7.1 %collective-permute-done.11.refs_5_ = bf16[16,128,128]{2,1,0:T(8,128)(2,1)S(1)} collective-permute-done((bf16[16,128,128]{2,1,0:T(8,128)(2,1)S(1)}, bf16[16,128,128]{2,1,0:T(8,128)(2,1)S(1)}, u32[]{:S(2)}, u32[]{:S(2)}) %collective-permute-start.11) | collective-permute-done | bytes 524320 | tf_op jit(solution)/shard_map/ppermute | solution.py:35
  61.4 3.4 %gather_products.1.own_ref = f32[2,128,128]{2,1,0:T(8,128)S(1)} custom-call(s32[128]{0:T(128)S(1)} %get-tuple-element.74.place_ref, s32[128]{0:T(128)S(1)} %get-tuple-element.75.slot_ref, bf16[128,128,128]{2,1,0:T(8,128)(2,1)S(1)} %cast_counts.1.counts_ref, bf16[16,128,128]{2,1,0:T(8,128)(2,1)S(1)} %constant_dynamic-update-slice_fusion.refs_0_, ...), custom_call_target="tpu_custom_call" | custom-call | flops 536870912 | bytes 8388608 | tf_op jit(solution)/shard_map/gather_products/pallas_call | solution.py:95
  68.0 5.2 %spread_terms.1 = (bf16[16,128,128]{2,1,0:T(8,128)(2,1)S(1)}, bf16[16,128,128]{2,1,0:T(8,128)(2,1)}, bf16[16,128,128]{2,1,0:T(8,128)(2,1)}, bf16[16,128,128]{2,1...) custom-call(s32[128]{0:T(128)S(1)} %get-tuple-element.72.place_ref, ...), custom_call_target="tpu_custom_call" | custom-call | flops 536870912 | bytes 8388608 | tf_op jit(solution)/shard_map/spread_terms/pallas_call | solution.py:162
  74.0 4.1 %collective-permute-start.19 = (bf16[16,128,128]{2,1,0:T(8,128)(2,1)S(1)}, bf16[16,128,128]{2,1,0:T(8,128)(2,1)S(1)}, u32[]{:S(2)}, u32[]{:S(2)}) collective-permute-start(bf16[16,128,128]{2,1,0:T(8,128)(2,1)S(1)} %get-tuple-element.57), channel_id=1, source_target_pairs={{0,6},{2,0},{4,2},{6,4},{8,14},{10,8},{12,10},{14,12},{16,22},{18,... | collective-permute-start | bytes 1572872 | tf_op jit(solution)/shard_map/ppermute | solution.py:35
  79.2 7.3 %all-to-all-start = ((f32[16,32,128]{2,1,0:T(8,128)}), f32[16,32,128]{2,1,0:T(8,128)}, u32[]{:S(2)}, u32[]{:S(2)}) async-start(f32[16,32,128]{2,1,0:T(8,128)} %bitcast.1), calls=%async_computation | async-start | bytes 524288 | tf_op jit(solution)/shard_map/all_to_all | solution.py:317
  88.1 2.4 %collective-permute-done.19.refs_1_ = bf16[16,128,128]{2,1,0:T(8,128)(2,1)S(1)} collective-permute-done((bf16[16,128,128]{2,1,0:T(8,128)(2,1)S(1)}, bf16[16,128,128]{2,1,0:T(8,128)(2,1)S(1)}, u32[]{:S(2)}, u32[]{:S(2)}) %collective-permute-start.19) | collective-permute-done | bytes 524320 | tf_op jit(solution)/shard_map/ppermute | solution.py:35
  92.8 5.2 %collective-permute-done.21.refs_3_ = bf16[16,128,128]{2,1,0:T(8,128)(2,1)} collective-permute-done((bf16[16,128,128]{2,1,0:T(8,128)(2,1)}, bf16[16,128,128]{2,1,0:T(8,128)(2,1)}, u32[]{:S(2)}, u32[]{:S(2)}) %collective-permute-start.21) | collective-permute-done | bytes 524320 | tf_op jit(solution)/shard_map/ppermute | solution.py:35
  98.0 2.3 %class_sum.1 = bf16[16,128,128]{2,1,0:T(8,128)(2,1)} custom-call(bf16[16,128,128]{2,1,0:T(8,128)(2,1)S(1)} %get-tuple-element.56.refs_0_, bf16[16,128,128]{2,1,0:T(8,128)(2,1)S(1)} %collective-permute-done.19.refs_1_, bf16[16,128,128]{2,1,0:T(8,128)(2,1)} %collective-permute-done.20.refs_2_, bf16[16,128,128]{2,1,0:T(8,128)(2,1)} %collective-permute-done.21.refs_3_), custom_call_target="tpu_custom_call" | custom-call | tf_op jit(solution)/shard_map/class_sum/pallas_call | solution.py:188
  103.1 12.1 %all_to_all.10 = f32[16,32,128]{2,1,0:T(8,128)S(1)} all-to-all(f32[16,32,128]{2,1,0:T(8,128)S(1)} %broadcast_in_dim.124), channel_id=1, replica_groups=mesh['zq'=4,'zp'=2,'yq'=2,'yp'=2,'xq'=2,'xp'=2,'rep'=2] {'zp','yp','xp',..., dimensions={0} | all-to-all | bytes 524288 | tf_op jit(solution)/shard_map/all_to_all | solution.py:43
  115.6 3.9 %collective-permute-start.23 = (bf16[544,128]{1,0:T(8,128)(2,1)S(1)}, bf16[544,128]{1,0:T(8,128)(2,1)S(1)}, u32[]{:S(2)}, u32[]{:S(2)}) collective-permute-start(bf16[544,128]{1,0:T(8,128)(2,1)S(1)} %get-tuple-element.61), channel_id=1, source_target_pairs={{0,4},{2,6},{4,0},{6,2},{8,12},{10,14},{12,8},{14,10},{16,20},{18,... | collective-permute-start | bytes 417800 | tf_op jit(solution)/shard_map/ppermute | solution.py:35
  123.1 3.0 %collective-permute-done.24.refs_2_ = bf16[544,128]{1,0:T(8,128)(2,1)S(1)} collective-permute-done((bf16[544,128]{1,0:T(8,128)(2,1)S(1)}, bf16[544,128]{1,0:T(8,128)(2,1)S(1)}, u32[]{:S(2)}, u32[]{:S(2)}) %collective-permute-start.24) | collective-permute-done | bytes 139296 | tf_op jit(solution)/shard_map/ppermute | solution.py:35
  126.1 3.6 %collective-permute-done.25.refs_3_ = bf16[544,128]{1,0:T(8,128)(2,1)S(1)} collective-permute-done((bf16[544,128]{1,0:T(8,128)(2,1)S(1)}, bf16[544,128]{1,0:T(8,128)(2,1)S(1)}, u32[]{:S(2)}, u32[]{:S(2)}) %collective-permute-start.25) | collective-permute-done | bytes 139296 | tf_op jit(solution)/shard_map/ppermute | solution.py:35
  130.7 8.2 %collective-permute-start.27 = (bf16[256,128]{1,0:T(8,128)(2,1)S(1)}, bf16[256,128]{1,0:T(8,128)(2,1)S(1)}, u32[]{:S(2)}, u32[]{:S(2)}) collective-permute-start(bf16[256,128]{1,0:T(8,128)(2,1)S(1)} %get-tuple-element.66), channel_id=1, source_target_pairs={{0,128},{2,130},{4,132},{6,134},{8,136},{10,138},{12,140},{14,142}... | collective-permute-start | bytes 196616 | tf_op jit(solution)/shard_map/ppermute | solution.py:35
  140.1 2.5 %collective-permute-done.27.refs_2_ = bf16[256,128]{1,0:T(8,128)(2,1)S(1)} collective-permute-done((bf16[256,128]{1,0:T(8,128)(2,1)S(1)}, bf16[256,128]{1,0:T(8,128)(2,1)S(1)}, u32[]{:S(2)}, u32[]{:S(2)}) %collective-permute-start.27) | collective-permute-done | bytes 65568 | tf_op jit(solution)/shard_map/ppermute | solution.py:35
  (74 shorter events, 30.8 us)
Async XLA Ops:
  0.6 10.1 %collective-permute-start.2 = (bf16[1,128,128]{2,1,0:T(8,128)(2,1)}, bf16[1,128,128]{2,1,0:T(8,128)(2,1)S(1)}, u32[]{:S(2)}, u32[]{:S(2)}) collective-permute-start(bf16[1,128,128]{2,1,0:T(8,128)(2,1)} %bitcast.3), channel_id=1, source_target_pairs={{0,192},{2,194},{4,196},{6,198},{8,200},{10,202},{12,204},{14,206}... | collective-permute-start | bytes 98312 | tf_op jit(solution)/shard_map/ppermute | solution.py:35
  6.1 8.0 %collective-permute-start.1 = (bf16[1,128,128]{2,1,0:T(8,128)(2,1)}, bf16[1,128,128]{2,1,0:T(8,128)(2,1)S(1)}, u32[]{:S(2)}, u32[]{:S(2)}) collective-permute-start(bf16[1,128,128]{2,1,0:T(8,128)(2,1)} %bitcast.4), channel_id=1, source_target_pairs={{0,128},{2,130},{4,132},{6,134},{8,136},{10,138},{12,140},{14,142}... | collective-permute-start | bytes 98312 | tf_op jit(solution)/shard_map/ppermute | solution.py:35
  7.5 6.6 %collective-permute-start = (bf16[1,128,128]{2,1,0:T(8,128)(2,1)}, bf16[1,128,128]{2,1,0:T(8,128)(2,1)S(1)}, u32[]{:S(2)}, u32[]{:S(2)}) collective-permute-start(bf16[1,128,128]{2,1,0:T(8,128)(2,1)} %bitcast.5), channel_id=1, source_target_pairs={{0,64},{2,66},{4,68},{6,70},{8,72},{10,74},{12,76},{14,78},{16,80}... | collective-permute-start | bytes 98312 | tf_op jit(solution)/shard_map/ppermute | solution.py:35
  14.9 12.6 %collective-permute-start.5 = (bf16[4,128,128]{2,1,0:T(8,128)(2,1)S(1)}, bf16[4,128,128]{2,1,0:T(8,128)(2,1)S(1)}, u32[]{:S(2)}, u32[]{:S(2)}) collective-permute-start(bf16[4,128,128]{2,1,0:T(8,128)(2,1)S(1)} %pad_maximum_fusion), channel_id=1, source_target_pairs={{0,20},{2,22},{4,16},{6,18},{8,28},{10,30},{12,24},{14,26},{16,4},... | collective-permute-start | bytes 393224 | tf_op jit(solution)/shard_map/ppermute | solution.py:35
  20.7 6.8 %collective-permute-start.4 = (bf16[4,128,128]{2,1,0:T(8,128)(2,1)S(1)}, bf16[4,128,128]{2,1,0:T(8,128)(2,1)S(1)}, u32[]{:S(2)}, u32[]{:S(2)}) collective-permute-start(bf16[4,128,128]{2,1,0:T(8,128)(2,1)S(1)} %pad_maximum_fusion), channel_id=1, source_target_pairs={{0,16},{2,18},{4,20},{6,22},{8,24},{10,26},{12,28},{14,30},{16,0},... | collective-permute-start | bytes 393224 | tf_op jit(solution)/shard_map/ppermute | solution.py:35
  27.6 13.6 %collective-permute-start.8 = (bf16[16,128,128]{2,1,0:T(8,128)(2,1)S(1)}, bf16[16,128,128]{2,1,0:T(8,128)(2,1)S(1)}, u32[]{:S(2)}, u32[]{:S(2)}) collective-permute-start(bf16[16,128,128]{2,1,0:T(8,128)(2,1)S(1)} %constant_dynamic-update-slice_fusion.refs_0_), channel_id=1, source_target_pairs={{0,254},{2,248},{4,250},{6,252},{8,230},{10,224},{12,226},{14,228}... | collective-permute-start | bytes 1572872 | tf_op jit(solution)/shard_map/ppermute | solution.py:35
  31.8 15.9 %collective-permute-start.10 = (bf16[16,128,128]{2,1,0:T(8,128)(2,1)S(1)}, bf16[16,128,128]{2,1,0:T(8,128)(2,1)S(1)}, u32[]{:S(2)}, u32[]{:S(2)}) collective-permute-start(bf16[16,128,128]{2,1,0:T(8,128)(2,1)S(1)} %constant_dynamic-update-slice_fusion.refs_0_), channel_id=1, source_target_pairs={{0,32},{2,34},{4,36},{6,38},{8,40},{10,42},{12,44},{14,46},{16,48}... | collective-permute-start | bytes 1572872 | tf_op jit(solution)/shard_map/ppermute | solution.py:35
  33.4 20.9 %collective-permute-start.7 = (bf16[16,128,128]{2,1,0:T(8,128)(2,1)S(1)}, bf16[16,128,128]{2,1,0:T(8,128)(2,1)S(1)}, u32[]{:S(2)}, u32[]{:S(2)}) collective-permute-start(bf16[16,128,128]{2,1,0:T(8,128)(2,1)S(1)} %constant_dynamic-update-slice_fusion.refs_0_), channel_id=1, source_target_pairs={{0,8},{2,10},{4,12},{6,14},{8,16},{10,18},{12,20},{14,22},{16,24},... | collective-permute-start | bytes 1572872 | tf_op jit(solution)/shard_map/ppermute | solution.py:35
  33.4 20.9 %collective-permute-start.6 = (bf16[16,128,128]{2,1,0:T(8,128)(2,1)S(1)}, bf16[16,128,128]{2,1,0:T(8,128)(2,1)S(1)}, u32[]{:S(2)}, u32[]{:S(2)}) collective-permute-start(bf16[16,128,128]{2,1,0:T(8,128)(2,1)S(1)} %constant_dynamic-update-slice_fusion.refs_0_), channel_id=1, source_target_pairs={{0,2},{2,4},{4,6},{6,0},{8,10},{10,12},{12,14},{14,8},{16,18},{18,... | collective-permute-start | bytes 1572872 | tf_op jit(solution)/shard_map/ppermute | solution.py:35
  41.1 13.1 %collective-permute-start.12 = (bf16[16,128,128]{2,1,0:T(8,128)(2,1)S(1)}, bf16[16,128,128]{2,1,0:T(8,128)(2,1)S(1)}, u32[]{:S(2)}, u32[]{:S(2)}) collective-permute-start(bf16[16,128,128]{2,1,0:T(8,128)(2,1)S(1)} %collective-permute-done.8.refs_7_), channel_id=1, source_target_pairs={{0,6},{2,0},{4,2},{6,4},{8,14},{10,8},{12,10},{14,12},{16,22},{18,... | collective-permute-start | bytes 1572872 | tf_op jit(solution)/shard_map/ppermute | solution.py:35
  43.8 17.6 %collective-permute-start.11 = (bf16[16,128,128]{2,1,0:T(8,128)(2,1)S(1)}, bf16[16,128,128]{2,1,0:T(8,128)(2,1)S(1)}, u32[]{:S(2)}, u32[]{:S(2)}) collective-permute-start(bf16[16,128,128]{2,1,0:T(8,128)(2,1)S(1)} %collective-permute-done.8.refs_7_), channel_id=1, source_target_pairs={{0,24},{2,26},{4,28},{6,30},{8,0},{10,2},{12,4},{14,6},{16,8},{18,... | collective-permute-start | bytes 1572872 | tf_op jit(solution)/shard_map/ppermute | solution.py:35
  47.7 13.7 %collective-permute-start.9 = (bf16[16,128,128]{2,1,0:T(8,128)(2,1)S(1)}, bf16[16,128,128]{2,1,0:T(8,128)(2,1)S(1)}, u32[]{:S(2)}, u32[]{:S(2)}) collective-permute-start(bf16[16,128,128]{2,1,0:T(8,128)(2,1)S(1)} %collective-permute-done.8.refs_7_), channel_id=1, source_target_pairs={{0,224},{2,226},{4,228},{6,230},{8,232},{10,234},{12,236},{14,238}... | collective-permute-start | bytes 1572872 | tf_op jit(solution)/shard_map/ppermute | solution.py:35
  74.0 16.5 %collective-permute-start.19 = (bf16[16,128,128]{2,1,0:T(8,128)(2,1)S(1)}, bf16[16,128,128]{2,1,0:T(8,128)(2,1)S(1)}, u32[]{:S(2)}, u32[]{:S(2)}) collective-permute-start(bf16[16,128,128]{2,1,0:T(8,128)(2,1)S(1)} %get-tuple-element.57), channel_id=1, source_target_pairs={{0,6},{2,0},{4,2},{6,4},{8,14},{10,8},{12,10},{14,12},{16,22},{18,... | collective-permute-start | bytes 1572872 | tf_op jit(solution)/shard_map/ppermute | solution.py:35
  78.0 14.7 %collective-permute-start.20 = (bf16[16,128,128]{2,1,0:T(8,128)(2,1)}, bf16[16,128,128]{2,1,0:T(8,128)(2,1)}, u32[]{:S(2)}, u32[]{:S(2)}) collective-permute-start(bf16[16,128,128]{2,1,0:T(8,128)(2,1)} %get-tuple-element.58), channel_id=1, source_target_pairs={{0,24},{2,26},{4,28},{6,30},{8,0},{10,2},{12,4},{14,6},{16,8},{18,... | collective-permute-start | bytes 1572872 | tf_op jit(solution)/shard_map/ppermute | solution.py:35
  79.2 18.8 %collective-permute-start.21 = (bf16[16,128,128]{2,1,0:T(8,128)(2,1)}, bf16[16,128,128]{2,1,0:T(8,128)(2,1)}, u32[]{:S(2)}, u32[]{:S(2)}) collective-permute-start(bf16[16,128,128]{2,1,0:T(8,128)(2,1)} %get-tuple-element.59), channel_id=1, source_target_pairs={{0,224},{2,226},{4,228},{6,230},{8,232},{10,234},{12,236},{14,238}... | collective-permute-start | bytes 1572872 | tf_op jit(solution)/shard_map/ppermute | solution.py:35
  79.2 22.9 %all-to-all-start = ((f32[16,32,128]{2,1,0:T(8,128)}), f32[16,32,128]{2,1,0:T(8,128)}, u32[]{:S(2)}, u32[]{:S(2)}) async-start(f32[16,32,128]{2,1,0:T(8,128)} %bitcast.1), calls=%async_computation | async-start | bytes 524288 | tf_op jit(solution)/shard_map/all_to_all | solution.py:317
  86.5 28.7 %collective-permute-start.16 = (bf16[16,128,128]{2,1,0:T(8,128)(2,1)}, bf16[16,128,128]{2,1,0:T(8,128)(2,1)S(1)}, u32[]{:S(2)}, u32[]{:S(2)}) collective-permute-start(bf16[16,128,128]{2,1,0:T(8,128)(2,1)} %get-tuple-element.53), channel_id=1, source_target_pairs={{0,2},{2,4},{4,6},{6,0},{8,10},{10,12},{12,14},{14,8},{16,18},{18,... | collective-permute-start | bytes 1572872 | tf_op jit(solution)/shard_map/ppermute | solution.py:35
  87.3 27.9 %collective-permute-start.17 = (bf16[16,128,128]{2,1,0:T(8,128)(2,1)}, bf16[16,128,128]{2,1,0:T(8,128)(2,1)S(1)}, u32[]{:S(2)}, u32[]{:S(2)}) collective-permute-start(bf16[16,128,128]{2,1,0:T(8,128)(2,1)} %get-tuple-element.54), channel_id=1, source_target_pairs={{0,8},{2,10},{4,12},{6,14},{8,16},{10,18},{12,20},{14,22},{16,24},... | collective-permute-start | bytes 1572872 | tf_op jit(solution)/shard_map/ppermute | solution.py:35
  90.4 24.8 %collective-permute-start.18 = (bf16[16,128,128]{2,1,0:T(8,128)(2,1)}, bf16[16,128,128]{2,1,0:T(8,128)(2,1)S(1)}, u32[]{:S(2)}, u32[]{:S(2)}) collective-permute-start(bf16[16,128,128]{2,1,0:T(8,128)(2,1)} %copy-done.4), channel_id=1, source_target_pairs={{0,32},{2,34},{4,36},{6,38},{8,40},{10,42},{12,44},{14,46},{16,48}... | collective-permute-start | bytes 1572872 | tf_op jit(solution)/shard_map/ppermute | solution.py:35
  100.3 14.9 %collective-permute-start.22 = (bf16[16,128,128]{2,1,0:T(8,128)(2,1)}, bf16[16,128,128]{2,1,0:T(8,128)(2,1)S(1)}, u32[]{:S(2)}, u32[]{:S(2)}) collective-permute-start(bf16[16,128,128]{2,1,0:T(8,128)(2,1)} %class_sum.1), channel_id=1, source_target_pairs={{0,254},{2,248},{4,250},{6,252},{8,230},{10,224},{12,226},{14,228}... | collective-permute-start | bytes 1572872 | tf_op jit(solution)/shard_map/ppermute | solution.py:35
  115.6 7.5 %collective-permute-start.23 = (bf16[544,128]{1,0:T(8,128)(2,1)S(1)}, bf16[544,128]{1,0:T(8,128)(2,1)S(1)}, u32[]{:S(2)}, u32[]{:S(2)}) collective-permute-start(bf16[544,128]{1,0:T(8,128)(2,1)S(1)} %get-tuple-element.61), channel_id=1, source_target_pairs={{0,4},{2,6},{4,0},{6,2},{8,12},{10,14},{12,8},{14,10},{16,20},{18,... | collective-permute-start | bytes 417800 | tf_op jit(solution)/shard_map/ppermute | solution.py:35
  120.7 9.0 %collective-permute-start.25 = (bf16[544,128]{1,0:T(8,128)(2,1)S(1)}, bf16[544,128]{1,0:T(8,128)(2,1)S(1)}, u32[]{:S(2)}, u32[]{:S(2)}) collective-permute-start(bf16[544,128]{1,0:T(8,128)(2,1)S(1)} %get-tuple-element.63), channel_id=1, source_target_pairs={{0,20},{2,22},{4,16},{6,18},{8,28},{10,30},{12,24},{14,26},{16,4},... | collective-permute-start | bytes 417800 | tf_op jit(solution)/shard_map/ppermute | solution.py:35
  129.7 10.4 %collective-permute-start.26 = (bf16[256,128]{1,0:T(8,128)(2,1)S(1)}, bf16[256,128]{1,0:T(8,128)(2,1)S(1)}, u32[]{:S(2)}, u32[]{:S(2)}) collective-permute-start(bf16[256,128]{1,0:T(8,128)(2,1)S(1)} %get-tuple-element.65), channel_id=1, source_target_pairs={{0,64},{2,66},{4,68},{6,70},{8,72},{10,74},{12,76},{14,78},{16,80}... | collective-permute-start | bytes 196616 | tf_op jit(solution)/shard_map/ppermute | solution.py:35
  130.7 11.9 %collective-permute-start.27 = (bf16[256,128]{1,0:T(8,128)(2,1)S(1)}, bf16[256,128]{1,0:T(8,128)(2,1)S(1)}, u32[]{:S(2)}, u32[]{:S(2)}) collective-permute-start(bf16[256,128]{1,0:T(8,128)(2,1)S(1)} %get-tuple-element.66), channel_id=1, source_target_pairs={{0,128},{2,130},{4,132},{6,134},{8,136},{10,138},{12,140},{14,142}... | collective-permute-start | bytes 196616 | tf_op jit(solution)/shard_map/ppermute | solution.py:35
  (12 other events, 76.9 us)

commit v3 on v2

--- a/solution.py
+++ b/solution.py
@@ -11,10 +11,12 @@
 edge_moment = 14.0 / 96.0
 f32, bf16 = jnp.float32, jnp.bfloat16
 CHUNK = 16
+UNROLL = 8
+NEAR, FAR = (0, 1, 2, 4, 7), (3, 5, 6)
 HIGH, LOW = ("zq", "yq", "xq"), ("zp", "yp", "xp", "rep")
 ROWS = ("zq", "zp", "yq", "yp", "xq", "xp")
 ALL = ROWS + ("rep",)
-VMEM_LIMIT = 24 * 2**20
+VMEM_LIMIT = 16 * 2**20
 SMEM = pl.BlockSpec(memory_space=pltpu.SMEM)
 VMEM = pl.BlockSpec(memory_space=pltpu.VMEM)
 def params():
@@ -57,7 +59,7 @@
 
 
 def cast_kernel(in_ref, out_ref):
-    out_ref[...] = in_ref[...].astype(f32).astype(bf16)
+    out_ref[...] = in_ref[...].astype(jnp.int8)
 
 
 def cast_counts(tile_counts):
@@ -65,43 +67,55 @@
     spec = pl.BlockSpec((CHUNK, block, block), lambda i: (i, 0, 0))
     return pl.pallas_call(
         cast_kernel,
-        out_shape=jax.ShapeDtypeStruct(tile_counts.shape, bf16),
+        out_shape=jax.ShapeDtypeStruct(tile_counts.shape, jnp.int8),
         grid=(tiles // CHUNK,),
         in_specs=[spec],
         out_specs=spec,
         compiler_params=params(),
-        cost_estimate=pl.CostEstimate(flops=tile_counts.size, bytes_accessed=tile_counts.size * 6, transcendentals=0),
+        cost_estimate=pl.CostEstimate(flops=tile_counts.size, bytes_accessed=tile_counts.size * 5, transcendentals=0),
         name="cast_counts",
     )(tile_counts)
 
 
-def gather_kernel(place_ref, slot_ref, counts_ref, *refs):
-    parts, (out_ref, held_ref) = refs[:8], refs[8:]
-    for k, part in enumerate(parts):
-        held_ref[16 * k : 16 * k + 16] = part[...]
-    out_ref[...] = jnp.zeros_like(out_ref)
-
-    @pl.loop(0, counts_ref.shape[0] // CHUNK)
-    def _(step):
-        for k in range(CHUNK):
-            tile = step * CHUNK + k
-            product = jnp.dot(counts_ref[tile], held_ref[place_ref[tile]], preferred_element_type=f32)
-            out_ref[slot_ref[tile]] += product
-
-
-def gather_products(place, slot, counts, parts):
+def for_tiles(far, rounds_ref, work_ref, body):
+    start, stop = (rounds_ref[0], rounds_ref[1]) if far else (0, rounds_ref[0])
+
+    def several(step, carry):
+        for k in range(UNROLL):
+            work = work_ref[step * UNROLL + k]
+            body(work & 127, work >> 7 & 255, work >> 15 & 255, work >> 23)
+        return carry
+
+    lax.fori_loop(start, stop, several, 0)
+
+
+def gather_kernel(far, rounds_ref, work_ref, counts_ref, *refs):
+    codes = FAR if far else NEAR
+    parts, (out_ref, held_ref) = refs[: len(codes)], refs[-2:]
+    for code, part in zip(codes, parts):
+        held_ref[16 * code : 16 * code + 16] = part[...]
+    held_ref[128] = jnp.zeros_like(held_ref[128])
+    out_ref[...] = refs[len(codes)][...] if far else jnp.zeros_like(out_ref)
+
+    def body(tile, source, target, slot):
+        out_ref[slot] += jnp.dot(counts_ref[tile].astype(f32).astype(bf16), held_ref[source], preferred_element_type=f32)
+
+    for_tiles(far, rounds_ref, work_ref, body)
+
+
+def gather_products(far, rounds, work, counts, parts, *before):
     tiles, block, _ = counts.shape
     width = parts[0].shape[-1]
     return pl.pallas_call(
-        gather_kernel,
+        functools.partial(gather_kernel, far),
         out_shape=jax.ShapeDtypeStruct((2, block, width), f32),
-        in_specs=[SMEM] * 2 + [VMEM] * 9,
+        in_specs=[SMEM] * 2 + [VMEM] * (1 + len(parts) + len(before)),
         out_specs=VMEM,
-        scratch_shapes=[pltpu.VMEM((128, block, width), bf16)],
-        compiler_params=params(),
-        cost_estimate=pl.CostEstimate(flops=2 * tiles * block**3, bytes_accessed=counts.size * 4, transcendentals=0),
-        name="gather_products",
-    )(place, slot, counts, *parts)
+        scratch_shapes=[pltpu.VMEM((129, block, width), bf16)],
+        compiler_params=params(),
+        cost_estimate=pl.CostEstimate(flops=2 * tiles * block**3, bytes_accessed=counts.size * 2, transcendentals=0),
+        name="far_products" if far else "near_products",
+    )(rounds, work, counts, *parts, *before)
 
 
 def dense_kernel(
@@ -140,35 +154,36 @@
                 grad_ref[2 * k], grad_ref[2 * k + 1] = grad[:, :128], grad[:, 128:]
 
 
-def spread_kernel(place_ref, slot_ref, counts_ref, back_ref, *refs):
-    outs, held_ref = refs[:8], refs[8]
-    held_ref[...] = jnp.zeros_like(held_ref)
-
-    @pl.loop(0, counts_ref.shape[0] // CHUNK)
-    def _(step):
-        for k in range(CHUNK):
-            tile = step * CHUNK + k
-            term = jnp.dot(back_ref[slot_ref[tile]], counts_ref[tile], preferred_element_type=f32).astype(bf16)
-            place = place_ref[tile]
-            held_ref[place] = (held_ref[place].astype(f32) + term.astype(f32)).astype(bf16)
-
-    for k, out in enumerate(outs):
-        out[...] = held_ref[16 * k : 16 * k + 16]
-
-
-def spread_terms(place, slot, counts, back):
+def spread_kernel(far, rounds_ref, work_ref, counts_ref, back_ref, *refs):
+    codes = FAR if far else NEAR
+    outs, held_ref = refs[:-1], refs[-1]
+    for code in codes:
+        held_ref[16 * code : 16 * code + 16] = jnp.zeros_like(outs[0])
+    held_ref[128] = jnp.zeros_like(held_ref[128])
+
+    def body(tile, source, target, slot):
+        term = jnp.dot(back_ref[slot], counts_ref[tile].astype(f32).astype(bf16), preferred_element_type=f32).astype(bf16)
+        held_ref[target] = (held_ref[target].astype(f32) + term.astype(f32)).astype(bf16)
+
+    for_tiles(far, rounds_ref, work_ref, body)
+    for code, out in zip(codes, outs):
+        out[...] = held_ref[16 * code : 16 * code + 16]
+
+
+def spread_terms(far, rounds, work, counts, back):
     tiles, block, _ = counts.shape
     width = back.shape[1]
-    return pl.pallas_call(
-        spread_kernel,
-        out_shape=[jax.ShapeDtypeStruct((16, width, block), bf16)] * 8,
+    outs = len(FAR if far else NEAR)
+    return pl.pallas_call(
+        functools.partial(spread_kernel, far),
+        out_shape=[jax.ShapeDtypeStruct((16, width, block), bf16)] * outs,
         in_specs=[SMEM] * 2 + [VMEM] * 2,
-        out_specs=[VMEM] * 8,
-        scratch_shapes=[pltpu.VMEM((128, width, block), bf16)],
-        compiler_params=params(),
-        cost_estimate=pl.CostEstimate(flops=2 * tiles * block**3, bytes_accessed=counts.size * 4, transcendentals=0),
-        name="spread_terms",
-    )(place, slot, counts, back)
+        out_specs=[VMEM] * outs,
+        scratch_shapes=[pltpu.VMEM((129, width, block), bf16)],
+        compiler_params=params(),
+        cost_estimate=pl.CostEstimate(flops=2 * tiles * block**3, bytes_accessed=counts.size * 2, transcendentals=0),
+        name="far_terms" if far else "near_terms",
+    )(rounds, work, counts, back)
 
 
 def add_up(refs, index):
@@ -251,21 +266,16 @@
         ref[k % 4 * 32 : k % 4 * 32 + 32, k // 4 % 2 * 128 : k // 4 % 2 * 128 + 128] = cells_ref[k]
 
 
-def gather_blocks(features, tile_counts):
+def gather_blocks(features, tile_counts, *ready):
     own = features[None]
     own = jnp.concatenate([own, move(own, 2, 0, 0), move(own, 4, 0, 0), move(own, -2, 0, 0)])
     own = jnp.concatenate([own, move(own, 0, 0, 2), move(own, 0, 2, 0), move(own, 0, 2, 2)])
     own, tile_counts = lax.optimization_barrier((own, tile_counts))
     far = move(own, -1, -1, -1)
-    by_x, by_y, by_z = move(own, 0, 0, 1), move(own, 0, 1, 0), move(own, 1, 0, 0)
-    parts = [own, by_x, by_y, move(far, -1, 0, 0), by_z, move(far, 0, -1, 0), move(far, 0, 0, -1), far]
-    return parts, tile_counts
-
-
-def reduce_blocks(terms):
-    far = class_sum([terms[7], move(terms[6], 0, 0, -1), move(terms[5], 0, -1, 0), move(terms[3], -1, 0, 0)])
-    direct = [move(terms[1], 0, 0, 1), move(terms[2], 0, 1, 0), move(terms[4], 1, 0, 0)]
-    return [terms[0], *direct, move(far, -1, -1, -1)]
+    counts = cast_counts(tile_counts)
+    far, counts, *ready = lax.optimization_barrier((far, counts, *ready))
+    near = [own, move(own, 0, 0, 1), move(own, 0, 1, 0), move(own, 1, 0, 0), far]
+    return near, [move(far, -1, 0, 0), move(far, 0, -1, 0), move(far, 0, 0, -1)], counts, *ready
 
 
 def shards(
@@ -279,22 +289,34 @@
     scale = (edge_moment * tile_total * reps * block / 2) ** (-0.5)
     swap = [(0, 1), (1, 0)]
 
-    owner, here = tile_col // reps, lax.axis_index(ROWS)
+    owner, here = tile_col >> 1, lax.axis_index(ROWS)
     source, target = place_of(owner, here), place_of(here, owner)
     step = jnp.arange(16, dtype=jnp.int32)
-    order = (here // 32 - step % 4) % 4 * 4 + (here // 8 + step // 8) % 2 * 2 + (here // 2 + step // 4) % 2
+    order = ((here >> 5) - step & 3) * 4 + ((here >> 3) + (step >> 3) & 1) * 2 + ((here >> 1) + (step >> 2) & 1)
     slot = jnp.bitwise_xor(tile_row, rep)
-
-    gathered, tile_counts = gather_blocks(features, tile_counts)
-    counts = cast_counts(tile_counts)
+    tiles = jnp.arange(tile_total, dtype=jnp.int32)
+    near_tile = functools.reduce(jnp.logical_and, [source // 16 != code for code in FAR])
+    before = tiles[None, :] < tiles[:, None]
+    rank = jnp.sum(before & (near_tile[None, :] == near_tile[:, None]), axis=1, dtype=jnp.int32)
+    near_rounds = jnp.sum(near_tile, dtype=jnp.int32) + UNROLL - 1 >> 3
+    far_rounds = jnp.sum(~near_tile, dtype=jnp.int32) + UNROLL - 1 >> 3
+    rounds = jnp.stack([near_rounds, near_rounds + far_rounds])
+    rank = jnp.where(near_tile, rank, near_rounds * UNROLL + rank)
+    unused = 128 * 2**7 + 128 * 2**15
+    work = tiles + source * 2**7 + target * 2**15 + slot * 2**23 - unused
+    entries = jnp.arange(tile_total + 2 * UNROLL, dtype=jnp.int32)
+    work = unused + jnp.sum(jnp.where(rank[None, :] == entries[:, None], work[None, :], 0), axis=1, dtype=jnp.int32)
 
     local_ids = label_ids % half_rows
     label_mask = jnp.any(local_ids[:, None] == jnp.arange(half_rows, dtype=jnp.int32)[None, :], axis=0)
     masked = jnp.where(label_mask[:, None], cotangent, jnp.zeros_like(cotangent))
+    near, far, counts, rounds, work, masked = gather_blocks(features, tile_counts, rounds, work, masked)
     features_other = lax.ppermute(features, "rep", swap)
     masked_other = lax.ppermute(masked, "rep", swap)
 
-    own = gather_products(source, slot, counts, gathered)
+    own = gather_products(False, rounds, work, counts, near)
+    own, features_other, masked_other = lax.optimization_barrier((own, features_other, masked_other))
+    own = gather_products(True, rounds, work, counts, far, own)
     other = lax.ppermute(own, "rep", swap)
 
     activation, back, own_term, grads = pl.pallas_call(
@@ -309,9 +331,12 @@
         name="dense",
     )(own, other, features, features_other, masked, masked_other, self_weight, neigh_weight)
 
-    terms = spread_terms(target, slot, counts, back)
-    *terms, grads = lax.optimization_barrier((*terms, grads))
-    parts = reduce_blocks(terms)
+    far = spread_terms(True, rounds, work, counts, back)
+    *far, grads = lax.optimization_barrier((*far, grads))
+    far = [move(far[0], -1, 0, 0), move(far[1], 0, -1, 0), move(far[2], 0, 0, -1)]
+    near = spread_terms(False, rounds, work, counts, back)
+    parts = [near[0], move(near[1], 0, 0, 1), move(near[2], 0, 1, 0), move(near[3], 1, 0, 0)]
+    parts.append(move(class_sum([near[4], *far]), -1, -1, -1))
 
     cells = grads.reshape(lax.axis_size(HIGH), -1, 128)
     cells = jnp.sum(lax.all_to_all(cells, HIGH, 0, 0, tiled=True), axis=0)

time: 146 us -> 139 us (0.952)
  waiting for transfers between devices: 46.7 us -> 32.3 us
  Pallas kernels: 14.3 us -> 18.7 us
  blocking collectives: 12.1 us -> 14 us
    ppermute x26, waiting for transfers between devices: 45.7 us -> 31 us  [move(): return lax.ppermute(block, ROWS, pairs)]
    pallas_call x2 -> x4, Pallas kernels: 8.59 us -> 13 us  [the longest x2 7.94 us: spread_terms(): pl.pallas_call(functools.partial(spread_kernel, far), out_shape=[jax.Shap...]
    all_to_all x1, blocking collectives: 12.1 us -> 14 us  [spread(): return lax.all_to_all(copies, axes, 0, 0, tiled=True)]
    unnamed x18 -> x14, local copies, waits for them, and re-layouts: 5.04 us -> 4.25 us
  transfers between devices with their start and end apart: 30 -> 30, of which waited for: 14 -> 10; matrix products, arithmetic and copies ran while one was open for 3% -> 3% of each run, Pallas kernels for 2% -> 7%
where the time goes in v3:
time: 139 us; the launch traced here: 138 us
  starting transfers between devices  62.6 us (45%)
  waiting for transfers between devices  32.3 us (23%)
  Pallas kernels  18.7 us (13%)
  blocking collectives  14 us (10%)
  local copies, waits for them, and re-layouts  4.29 us (3%)
  other arithmetic  4.23 us (3%)
  between operations  2.21 us (2%)
    ppermute x26, starting transfers between devices, move(): return lax.ppermute(block, ROWS, pairs)  56 us
    ppermute x26, waiting for transfers between devices, move(): return lax.ppermute(block, ROWS, pairs)  31 us
    all_to_all x1, blocking collectives, spread(): return lax.all_to_all(copies, axes, 0, 0, tiled=True)  14 us
    pallas_call x2, Pallas kernels, spread_terms(): pl.pallas_call(functools.partial(spread_kernel, far), out_shape=[jax.Shap...  7.94 us
    all_to_all x1, starting transfers between devices, shards(): cells = jnp.sum(lax.all_to_all(cells, HIGH, 0, 0, tiled=True), axis=0)  5.8 us
    pallas_call x2, Pallas kernels, gather_products(): pl.pallas_call(functools.partial(gather_kernel, far), out_shape=jax.Shape...  5.09 us
    unnamed x14, local copies, waits for them, and re-layouts  4.25 us
  transfers between devices with their start and end apart: 30, of which 10 were waited for; matrix products, arithmetic and copies ran while one was open for 3% of the time, Pallas kernels for 7%

profile of v3, /device:TPU:32, one launch (start us, length us, event | category | flops | bytes accessed | tf_op | source)
XLA Modules:
  0.0 138.4 jit_solution(12367177491469469733)
XLA Ops:
  0.6 5.5 %collective-permute-start.2 = (bf16[1,128,128]{2,1,0:T(8,128)(2,1)}, bf16[1,128,128]{2,1,0:T(8,128)(2,1)S(1)}, u32[]{:S(2)}, u32[]{:S(2)}) collective-permute-start(bf16[1,128,128]{2,1,0:T(8,128)(2,1)} %bitcast.5), channel_id=1, source_target_pairs={{0,192},{2,194},{4,196},{6,198},{8,200},{10,202},{12,204},{14,206}... | collective-permute-start | bytes 98312 | tf_op jit(solution)/shard_map/ppermute | solution.py:37
  15.3 5.7 %collective-permute-start.5 = (bf16[4,128,128]{2,1,0:T(8,128)(2,1)S(1)}, bf16[4,128,128]{2,1,0:T(8,128)(2,1)S(1)}, u32[]{:S(2)}, u32[]{:S(2)}) collective-permute-start(bf16[4,128,128]{2,1,0:T(8,128)(2,1)S(1)} %pad_maximum_fusion), channel_id=1, source_target_pairs={{0,20},{2,22},{4,16},{6,18},{8,28},{10,30},{12,24},{14,26},{16,4},... | collective-permute-start | bytes 393224 | tf_op jit(solution)/shard_map/ppermute | solution.py:37
  21.9 5.9 %collective-permute-done.3 = bf16[4,128,128]{2,1,0:T(8,128)(2,1)S(1)} collective-permute-done((bf16[4,128,128]{2,1,0:T(8,128)(2,1)S(1)}, bf16[4,128,128]{2,1,0:T(8,128)(2,1)S(1)}, u32[]{:S(2)}, u32[]{:S(2)}) %collective-permute-start.3) | collective-permute-done | bytes 131104 | tf_op jit(solution)/shard_map/ppermute | solution.py:37
  30.2 2.8 %collective-permute-start.6 = (bf16[16,128,128]{2,1,0:T(8,128)(2,1)S(1)}, bf16[16,128,128]{2,1,0:T(8,128)(2,1)S(1)}, u32[]{:S(2)}, u32[]{:S(2)}) collective-permute-start(bf16[16,128,128]{2,1,0:T(8,128)(2,1)S(1)} %constant_dynamic-update-slice_fusion.refs_0_), channel_id=1, source_target_pairs={{0,254},{2,248},{4,250},{6,252},{8,230},{10,224},{12,226},{14,228}... | collective-permute-start | bytes 1572872 | tf_op jit(solution)/shard_map/ppermute | solution.py:37
  35.1 3.4 %copy-done = s32[128,128,128]{2,1,0:T(8,128)S(1)} copy-done((s32[128,128,128]{2,1,0:T(8,128)S(1)}, s32[128,128,128]{2,1,0:T(8,128)}, u32[]{:S(2)}) %copy-start) | copy-done | bytes 8388632
  39.0 4.5 %collective-permute-done.6.refs_4_ = bf16[16,128,128]{2,1,0:T(8,128)(2,1)S(1)} collective-permute-done((bf16[16,128,128]{2,1,0:T(8,128)(2,1)S(1)}, bf16[16,128,128]{2,1,0:T(8,128)(2,1)S(1)}, u32[]{:S(2)}, u32[]{:S(2)}) %collective-permute-start.6) | collective-permute-done | bytes 524320 | tf_op jit(solution)/shard_map/ppermute | solution.py:37
  43.4 4.0 %collective-permute-start.9 = (bf16[16,128,128]{2,1,0:T(8,128)(2,1)S(1)}, bf16[16,128,128]{2,1,0:T(8,128)(2,1)S(1)}, u32[]{:S(2)}, u32[]{:S(2)}) collective-permute-start(bf16[16,128,128]{2,1,0:T(8,128)(2,1)S(1)} %collective-permute-done.6.refs_4_), channel_id=1, source_target_pairs={{0,6},{2,0},{4,2},{6,4},{8,14},{10,8},{12,10},{14,12},{16,22},{18,... | collective-permute-start | bytes 1572872 | tf_op jit(solution)/shard_map/ppermute | solution.py:37
  47.4 3.0 %collective-permute-start.8 = (bf16[16,128,128]{2,1,0:T(8,128)(2,1)S(1)}, bf16[16,128,128]{2,1,0:T(8,128)(2,1)S(1)}, u32[]{:S(2)}, u32[]{:S(2)}) collective-permute-start(bf16[16,128,128]{2,1,0:T(8,128)(2,1)S(1)} %collective-permute-done.6.refs_4_), channel_id=1, source_target_pairs={{0,24},{2,26},{4,28},{6,30},{8,0},{10,2},{12,4},{14,6},{16,8},{18,... | collective-permute-start | bytes 1572872 | tf_op jit(solution)/shard_map/ppermute | solution.py:37
  51.0 3.0 %near_products.1.refs_3_ = f32[2,128,128]{2,1,0:T(8,128)S(1)} custom-call(s32[2]{0:T(128)S(1)} %pad_add_fusion.rounds_ref, s32[144]{0:T(256)S(1)} %broadcast_add_fusion.work_ref, s8[128,128,128]{2,1,0:T(32,128)(4,1)S(1)} %cast_counts.1.counts_ref, bf16[16,128,128]{2,1,0:T(8,128)(2,1)S(1)} %constant_dynamic-update-slice_fusion.refs_0_, ...), custom_call_target="tpu_custom_call" | custom-call | flops 536870912 | bytes 4194304 | tf_op jit(solution)/shard_map/near_products/pallas_call | solution.py:109
  54.1 2.5 %collective-permute-done.9.refs_2_ = bf16[16,128,128]{2,1,0:T(8,128)(2,1)S(1)} collective-permute-done((bf16[16,128,128]{2,1,0:T(8,128)(2,1)S(1)}, bf16[16,128,128]{2,1,0:T(8,128)(2,1)S(1)}, u32[]{:S(2)}, u32[]{:S(2)}) %collective-permute-start.9) | collective-permute-done | bytes 524320 | tf_op jit(solution)/shard_map/ppermute | solution.py:37
  56.5 2.6 %collective-permute-done.8.refs_1_ = bf16[16,128,128]{2,1,0:T(8,128)(2,1)S(1)} collective-permute-done((bf16[16,128,128]{2,1,0:T(8,128)(2,1)S(1)}, bf16[16,128,128]{2,1,0:T(8,128)(2,1)S(1)}, u32[]{:S(2)}, u32[]{:S(2)}) %collective-permute-start.8) | collective-permute-done | bytes 524320 | tf_op jit(solution)/shard_map/ppermute | solution.py:37
  65.5 3.4 %far_terms.1 = (bf16[16,128,128]{2,1,0:T(8,128)(2,1)}, bf16[16,128,128]{2,1,0:T(8,128)(2,1)}, bf16[16,128,128]{2,1,0:T(8,128)(2,1)}) custom-call(s32[2]{0:T(128)S(1)} %pad_add_fusion.rounds_ref, s32[144]{0:T(256)S(1)} %broadcast_add_fusion.work_ref, s8[128,128,128]{2,1,0:T(32,128)(4,1)S(1)} %cast_counts.1.counts_ref, ...), custom_call_target="tpu_custom_call" | custom-call | flops 536870912 | bytes 4194304 | tf_op jit(solution)/shard_map/far_terms/pallas_call | solution.py:177
  71.0 5.8 %all-to-all-start = ((f32[16,32,128]{2,1,0:T(8,128)}), f32[16,32,128]{2,1,0:T(8,128)S(1)}, u32[]{:S(2)}, u32[]{:S(2)}) async-start(f32[16,32,128]{2,1,0:T(8,128)} %bitcast.3), calls=%async_computation | async-start | bytes 524288 | tf_op jit(solution)/shard_map/all_to_all | solution.py:342
  76.8 4.5 %near_terms.1 = (bf16[16,128,128]{2,1,0:T(8,128)(2,1)S(1)}, bf16[16,128,128]{2,1,0:T(8,128)(2,1)}, bf16[16,128,128]{2,1,0:T(8,128)(2,1)}, bf16[16,128,128]{2,1,0:T(8,128)(2,1)}, bf16[16,128,128]{2,1,0:T(8,128)(2,1)S(1)}) custom-call(s32[2]{0:T(128)S(1)} %pad_add_fusion.rounds_ref, s32[144]{0:T(256)S(1)} %broadcast_add_fusion.work_ref, ...), custom_call_target="tpu_custom_call" | custom-call | flops 536870912 | bytes 4194304 | tf_op jit(solution)/shard_map/near_terms/pallas_call | solution.py:177
  84.1 3.8 %collective-permute-start.18 = (bf16[16,128,128]{2,1,0:T(8,128)(2,1)}, bf16[16,128,128]{2,1,0:T(8,128)(2,1)S(1)}, u32[]{:S(2)}, u32[]{:S(2)}) collective-permute-start(bf16[16,128,128]{2,1,0:T(8,128)(2,1)} %get-tuple-element.61), channel_id=1, source_target_pairs={{0,32},{2,34},{4,36},{6,38},{8,40},{10,42},{12,44},{14,46},{16,48}... | collective-permute-start | bytes 1572872 | tf_op jit(solution)/shard_map/ppermute | solution.py:37
  90.2 3.2 %collective-permute-start.22 = (bf16[16,128,128]{2,1,0:T(8,128)(2,1)}, bf16[16,128,128]{2,1,0:T(8,128)(2,1)S(1)}, u32[]{:S(2)}, u32[]{:S(2)}) collective-permute-start(bf16[16,128,128]{2,1,0:T(8,128)(2,1)} %class_sum.1), channel_id=1, source_target_pairs={{0,254},{2,248},{4,250},{6,252},{8,230},{10,224},{12,226},{14,228}... | collective-permute-start | bytes 1572872 | tf_op jit(solution)/shard_map/ppermute | solution.py:37
  93.5 14.0 %all_to_all.10 = f32[16,32,128]{2,1,0:T(8,128)S(1)} all-to-all(f32[16,32,128]{2,1,0:T(8,128)S(1)} %broadcast_in_dim.148), channel_id=1, replica_groups=mesh['zq'=4,'zp'=2,'yq'=2,'yp'=2,'xq'=2,'xp'=2,'rep'=2] {'zp','yp','xp',..., dimensions={0} | all-to-all | bytes 524288 | tf_op jit(solution)/shard_map/all_to_all | solution.py:45
  107.9 3.6 %collective-permute-start.23 = (bf16[544,128]{1,0:T(8,128)(2,1)S(1)}, bf16[544,128]{1,0:T(8,128)(2,1)S(1)}, u32[]{:S(2)}, u32[]{:S(2)}) collective-permute-start(bf16[544,128]{1,0:T(8,128)(2,1)S(1)} %get-tuple-element.67), channel_id=1, source_target_pairs={{0,4},{2,6},{4,0},{6,2},{8,12},{10,14},{12,8},{14,10},{16,20},{18,... | collective-permute-start | bytes 417800 | tf_op jit(solution)/shard_map/ppermute | solution.py:37
  111.5 3.0 %collective-permute-start.24 = (bf16[544,128]{1,0:T(8,128)(2,1)S(1)}, bf16[544,128]{1,0:T(8,128)(2,1)S(1)}, u32[]{:S(2)}, u32[]{:S(2)}) collective-permute-start(bf16[544,128]{1,0:T(8,128)(2,1)S(1)} %get-tuple-element.68), channel_id=1, source_target_pairs={{0,16},{2,18},{4,20},{6,22},{8,24},{10,26},{12,28},{14,30},{16,0},... | collective-permute-start | bytes 417800 | tf_op jit(solution)/shard_map/ppermute | solution.py:37
  115.4 5.0 %collective-permute-done.24.refs_2_ = bf16[544,128]{1,0:T(8,128)(2,1)S(1)} collective-permute-done((bf16[544,128]{1,0:T(8,128)(2,1)S(1)}, bf16[544,128]{1,0:T(8,128)(2,1)S(1)}, u32[]{:S(2)}, u32[]{:S(2)}) %collective-permute-start.24) | collective-permute-done | bytes 139296 | tf_op jit(solution)/shard_map/ppermute | solution.py:37
  120.4 3.1 %collective-permute-done.25.refs_3_ = bf16[544,128]{1,0:T(8,128)(2,1)S(1)} collective-permute-done((bf16[544,128]{1,0:T(8,128)(2,1)S(1)}, bf16[544,128]{1,0:T(8,128)(2,1)S(1)}, u32[]{:S(2)}, u32[]{:S(2)}) %collective-permute-start.25) | collective-permute-done | bytes 139296 | tf_op jit(solution)/shard_map/ppermute | solution.py:37
  123.6 4.9 %collective-permute-start.26 = (bf16[256,128]{1,0:T(8,128)(2,1)S(1)}, bf16[256,128]{1,0:T(8,128)(2,1)S(1)}, u32[]{:S(2)}, u32[]{:S(2)}) collective-permute-start(bf16[256,128]{1,0:T(8,128)(2,1)S(1)} %get-tuple-element.71), channel_id=1, source_target_pairs={{0,64},{2,66},{4,68},{6,70},{8,72},{10,74},{12,76},{14,78},{16,80}... | collective-permute-start | bytes 196616 | tf_op jit(solution)/shard_map/ppermute | solution.py:37
  129.3 2.9 %collective-permute-start.28 = (bf16[256,128]{1,0:T(8,128)(2,1)S(1)}, bf16[256,128]{1,0:T(8,128)(2,1)S(1)}, u32[]{:S(2)}, u32[]{:S(2)}) collective-permute-start(bf16[256,128]{1,0:T(8,128)(2,1)S(1)} %get-tuple-element.73), channel_id=1, source_target_pairs={{0,192},{2,194},{4,196},{6,198},{8,200},{10,202},{12,204},{14,206}... | collective-permute-start | bytes 196616 | tf_op jit(solution)/shard_map/ppermute | solution.py:37
  132.1 5.0 %collective-permute-done.27.refs_2_ = bf16[256,128]{1,0:T(8,128)(2,1)S(1)} collective-permute-done((bf16[256,128]{1,0:T(8,128)(2,1)S(1)}, bf16[256,128]{1,0:T(8,128)(2,1)S(1)}, u32[]{:S(2)}, u32[]{:S(2)}) %collective-permute-start.27) | collective-permute-done | bytes 65568 | tf_op jit(solution)/shard_map/ppermute | solution.py:37
  (77 shorter events, 31.3 us)
Async XLA Ops:
  0.6 13.8 %collective-permute-start.2 = (bf16[1,128,128]{2,1,0:T(8,128)(2,1)}, bf16[1,128,128]{2,1,0:T(8,128)(2,1)S(1)}, u32[]{:S(2)}, u32[]{:S(2)}) collective-permute-start(bf16[1,128,128]{2,1,0:T(8,128)(2,1)} %bitcast.5), channel_id=1, source_target_pairs={{0,192},{2,194},{4,196},{6,198},{8,200},{10,202},{12,204},{14,206}... | collective-permute-start | bytes 98312 | tf_op jit(solution)/shard_map/ppermute | solution.py:37
  6.1 8.3 %collective-permute-start.1 = (bf16[1,128,128]{2,1,0:T(8,128)(2,1)}, bf16[1,128,128]{2,1,0:T(8,128)(2,1)S(1)}, u32[]{:S(2)}, u32[]{:S(2)}) collective-permute-start(bf16[1,128,128]{2,1,0:T(8,128)(2,1)} %bitcast.6), channel_id=1, source_target_pairs={{0,128},{2,130},{4,132},{6,134},{8,136},{10,138},{12,140},{14,142}... | collective-permute-start | bytes 98312 | tf_op jit(solution)/shard_map/ppermute | solution.py:37
  15.3 12.6 %collective-permute-start.5 = (bf16[4,128,128]{2,1,0:T(8,128)(2,1)S(1)}, bf16[4,128,128]{2,1,0:T(8,128)(2,1)S(1)}, u32[]{:S(2)}, u32[]{:S(2)}) collective-permute-start(bf16[4,128,128]{2,1,0:T(8,128)(2,1)S(1)} %pad_maximum_fusion), channel_id=1, source_target_pairs={{0,20},{2,22},{4,16},{6,18},{8,28},{10,30},{12,24},{14,26},{16,4},... | collective-permute-start | bytes 393224 | tf_op jit(solution)/shard_map/ppermute | solution.py:37
  27.9 22.5 %collective-permute-start.12 = (bf16[16,128,128]{2,1,0:T(8,128)(2,1)S(1)}, bf16[16,128,128]{2,1,0:T(8,128)(2,1)S(1)}, u32[]{:S(2)}, u32[]{:S(2)}) collective-permute-start(bf16[16,128,128]{2,1,0:T(8,128)(2,1)S(1)} %constant_dynamic-update-slice_fusion.refs_0_), channel_id=1, source_target_pairs={{0,32},{2,34},{4,36},{6,38},{8,40},{10,42},{12,44},{14,46},{16,48}... | collective-permute-start | bytes 1572872 | tf_op jit(solution)/shard_map/ppermute | solution.py:37
  30.2 13.2 %collective-permute-start.6 = (bf16[16,128,128]{2,1,0:T(8,128)(2,1)S(1)}, bf16[16,128,128]{2,1,0:T(8,128)(2,1)S(1)}, u32[]{:S(2)}, u32[]{:S(2)}) collective-permute-start(bf16[16,128,128]{2,1,0:T(8,128)(2,1)S(1)} %constant_dynamic-update-slice_fusion.refs_0_), channel_id=1, source_target_pairs={{0,254},{2,248},{4,250},{6,252},{8,230},{10,224},{12,226},{14,228}... | collective-permute-start | bytes 1572872 | tf_op jit(solution)/shard_map/ppermute | solution.py:37
  34.0 16.4 %collective-permute-start.11 = (bf16[16,128,128]{2,1,0:T(8,128)(2,1)S(1)}, bf16[16,128,128]{2,1,0:T(8,128)(2,1)S(1)}, u32[]{:S(2)}, u32[]{:S(2)}) collective-permute-start(bf16[16,128,128]{2,1,0:T(8,128)(2,1)S(1)} %constant_dynamic-update-slice_fusion.refs_0_), channel_id=1, source_target_pairs={{0,8},{2,10},{4,12},{6,14},{8,16},{10,18},{12,20},{14,22},{16,24},... | collective-permute-start | bytes 1572872 | tf_op jit(solution)/shard_map/ppermute | solution.py:37
  34.1 16.4 %collective-permute-start.10 = (bf16[16,128,128]{2,1,0:T(8,128)(2,1)S(1)}, bf16[16,128,128]{2,1,0:T(8,128)(2,1)S(1)}, u32[]{:S(2)}, u32[]{:S(2)}) collective-permute-start(bf16[16,128,128]{2,1,0:T(8,128)(2,1)S(1)} %constant_dynamic-update-slice_fusion.refs_0_), channel_id=1, source_target_pairs={{0,2},{2,4},{4,6},{6,0},{8,10},{10,12},{12,14},{14,8},{16,18},{18,... | collective-permute-start | bytes 1572872 | tf_op jit(solution)/shard_map/ppermute | solution.py:37
  43.4 13.1 %collective-permute-start.9 = (bf16[16,128,128]{2,1,0:T(8,128)(2,1)S(1)}, bf16[16,128,128]{2,1,0:T(8,128)(2,1)S(1)}, u32[]{:S(2)}, u32[]{:S(2)}) collective-permute-start(bf16[16,128,128]{2,1,0:T(8,128)(2,1)S(1)} %collective-permute-done.6.refs_4_), channel_id=1, source_target_pairs={{0,6},{2,0},{4,2},{6,4},{8,14},{10,8},{12,10},{14,12},{16,22},{18,... | collective-permute-start | bytes 1572872 | tf_op jit(solution)/shard_map/ppermute | solution.py:37
  47.4 11.7 %collective-permute-start.8 = (bf16[16,128,128]{2,1,0:T(8,128)(2,1)S(1)}, bf16[16,128,128]{2,1,0:T(8,128)(2,1)S(1)}, u32[]{:S(2)}, u32[]{:S(2)}) collective-permute-start(bf16[16,128,128]{2,1,0:T(8,128)(2,1)S(1)} %collective-permute-done.6.refs_4_), channel_id=1, source_target_pairs={{0,24},{2,26},{4,28},{6,30},{8,0},{10,2},{12,4},{14,6},{16,8},{18,... | collective-permute-start | bytes 1572872 | tf_op jit(solution)/shard_map/ppermute | solution.py:37
  50.4 10.3 %collective-permute-start.7 = (bf16[16,128,128]{2,1,0:T(8,128)(2,1)S(1)}, bf16[16,128,128]{2,1,0:T(8,128)(2,1)S(1)}, u32[]{:S(2)}, u32[]{:S(2)}) collective-permute-start(bf16[16,128,128]{2,1,0:T(8,128)(2,1)S(1)} %collective-permute-done.6.refs_4_), channel_id=1, source_target_pairs={{0,224},{2,226},{4,228},{6,230},{8,232},{10,234},{12,236},{14,238}... | collective-permute-start | bytes 1572872 | tf_op jit(solution)/shard_map/ppermute | solution.py:37
  69.0 15.1 %collective-permute-start.19 = (bf16[16,128,128]{2,1,0:T(8,128)(2,1)}, bf16[16,128,128]{2,1,0:T(8,128)(2,1)S(1)}, u32[]{:S(2)}, u32[]{:S(2)}) collective-permute-start(bf16[16,128,128]{2,1,0:T(8,128)(2,1)} %get-tuple-element.63), channel_id=1, source_target_pairs={{0,224},{2,226},{4,228},{6,230},{8,232},{10,234},{12,236},{14,238}... | collective-permute-start | bytes 1572872 | tf_op jit(solution)/shard_map/ppermute | solution.py:37
  69.8 18.1 %collective-permute-start.20 = (bf16[16,128,128]{2,1,0:T(8,128)(2,1)}, bf16[16,128,128]{2,1,0:T(8,128)(2,1)}, u32[]{:S(2)}, u32[]{:S(2)}) collective-permute-start(bf16[16,128,128]{2,1,0:T(8,128)(2,1)} %get-tuple-element.64), channel_id=1, source_target_pairs={{0,24},{2,26},{4,28},{6,30},{8,0},{10,2},{12,4},{14,6},{16,8},{18,... | collective-permute-start | bytes 1572872 | tf_op jit(solution)/shard_map/ppermute | solution.py:37
  70.9 16.9 %collective-permute-start.21 = (bf16[16,128,128]{2,1,0:T(8,128)(2,1)}, bf16[16,128,128]{2,1,0:T(8,128)(2,1)}, u32[]{:S(2)}, u32[]{:S(2)}) collective-permute-start(bf16[16,128,128]{2,1,0:T(8,128)(2,1)} %get-tuple-element.65), channel_id=1, source_target_pairs={{0,6},{2,0},{4,2},{6,4},{8,14},{10,8},{12,10},{14,12},{16,22},{18,... | collective-permute-start | bytes 1572872 | tf_op jit(solution)/shard_map/ppermute | solution.py:37
  71.0 22.4 %all-to-all-start = ((f32[16,32,128]{2,1,0:T(8,128)}), f32[16,32,128]{2,1,0:T(8,128)S(1)}, u32[]{:S(2)}, u32[]{:S(2)}) async-start(f32[16,32,128]{2,1,0:T(8,128)} %bitcast.3), calls=%async_computation | async-start | bytes 524288 | tf_op jit(solution)/shard_map/all_to_all | solution.py:342
  81.4 26.1 %collective-permute-start.16 = (bf16[16,128,128]{2,1,0:T(8,128)(2,1)}, bf16[16,128,128]{2,1,0:T(8,128)(2,1)S(1)}, u32[]{:S(2)}, u32[]{:S(2)}) collective-permute-start(bf16[16,128,128]{2,1,0:T(8,128)(2,1)} %get-tuple-element.59), channel_id=1, source_target_pairs={{0,2},{2,4},{4,6},{6,0},{8,10},{10,12},{12,14},{14,8},{16,18},{18,... | collective-permute-start | bytes 1572872 | tf_op jit(solution)/shard_map/ppermute | solution.py:37
  83.0 24.5 %collective-permute-start.17 = (bf16[16,128,128]{2,1,0:T(8,128)(2,1)}, bf16[16,128,128]{2,1,0:T(8,128)(2,1)S(1)}, u32[]{:S(2)}, u32[]{:S(2)}) collective-permute-start(bf16[16,128,128]{2,1,0:T(8,128)(2,1)} %get-tuple-element.60), channel_id=1, source_target_pairs={{0,8},{2,10},{4,12},{6,14},{8,16},{10,18},{12,20},{14,22},{16,24},... | collective-permute-start | bytes 1572872 | tf_op jit(solution)/shard_map/ppermute | solution.py:37
  84.1 23.4 %collective-permute-start.18 = (bf16[16,128,128]{2,1,0:T(8,128)(2,1)}, bf16[16,128,128]{2,1,0:T(8,128)(2,1)S(1)}, u32[]{:S(2)}, u32[]{:S(2)}) collective-permute-start(bf16[16,128,128]{2,1,0:T(8,128)(2,1)} %get-tuple-element.61), channel_id=1, source_target_pairs={{0,32},{2,34},{4,36},{6,38},{8,40},{10,42},{12,44},{14,46},{16,48}... | collective-permute-start | bytes 1572872 | tf_op jit(solution)/shard_map/ppermute | solution.py:37
  90.2 17.4 %collective-permute-start.22 = (bf16[16,128,128]{2,1,0:T(8,128)(2,1)}, bf16[16,128,128]{2,1,0:T(8,128)(2,1)S(1)}, u32[]{:S(2)}, u32[]{:S(2)}) collective-permute-start(bf16[16,128,128]{2,1,0:T(8,128)(2,1)} %class_sum.1), channel_id=1, source_target_pairs={{0,254},{2,248},{4,250},{6,252},{8,230},{10,224},{12,226},{14,228}... | collective-permute-start | bytes 1572872 | tf_op jit(solution)/shard_map/ppermute | solution.py:37
  107.9 7.5 %collective-permute-start.23 = (bf16[544,128]{1,0:T(8,128)(2,1)S(1)}, bf16[544,128]{1,0:T(8,128)(2,1)S(1)}, u32[]{:S(2)}, u32[]{:S(2)}) collective-permute-start(bf16[544,128]{1,0:T(8,128)(2,1)S(1)} %get-tuple-element.67), channel_id=1, source_target_pairs={{0,4},{2,6},{4,0},{6,2},{8,12},{10,14},{12,8},{14,10},{16,20},{18,... | collective-permute-start | bytes 417800 | tf_op jit(solution)/shard_map/ppermute | solution.py:37
  111.5 8.9 %collective-permute-start.24 = (bf16[544,128]{1,0:T(8,128)(2,1)S(1)}, bf16[544,128]{1,0:T(8,128)(2,1)S(1)}, u32[]{:S(2)}, u32[]{:S(2)}) collective-permute-start(bf16[544,128]{1,0:T(8,128)(2,1)S(1)} %get-tuple-element.68), channel_id=1, source_target_pairs={{0,16},{2,18},{4,20},{6,22},{8,24},{10,26},{12,28},{14,30},{16,0},... | collective-permute-start | bytes 417800 | tf_op jit(solution)/shard_map/ppermute | solution.py:37
  114.5 9.0 %collective-permute-start.25 = (bf16[544,128]{1,0:T(8,128)(2,1)S(1)}, bf16[544,128]{1,0:T(8,128)(2,1)S(1)}, u32[]{:S(2)}, u32[]{:S(2)}) collective-permute-start(bf16[544,128]{1,0:T(8,128)(2,1)S(1)} %get-tuple-element.69), channel_id=1, source_target_pairs={{0,20},{2,22},{4,16},{6,18},{8,28},{10,30},{12,24},{14,26},{16,4},... | collective-permute-start | bytes 417800 | tf_op jit(solution)/shard_map/ppermute | solution.py:37
  123.6 8.5 %collective-permute-start.26 = (bf16[256,128]{1,0:T(8,128)(2,1)S(1)}, bf16[256,128]{1,0:T(8,128)(2,1)S(1)}, u32[]{:S(2)}, u32[]{:S(2)}) collective-permute-start(bf16[256,128]{1,0:T(8,128)(2,1)S(1)} %get-tuple-element.71), channel_id=1, source_target_pairs={{0,64},{2,66},{4,68},{6,70},{8,72},{10,74},{12,76},{14,78},{16,80}... | collective-permute-start | bytes 196616 | tf_op jit(solution)/shard_map/ppermute | solution.py:37
  128.4 8.7 %collective-permute-start.27 = (bf16[256,128]{1,0:T(8,128)(2,1)S(1)}, bf16[256,128]{1,0:T(8,128)(2,1)S(1)}, u32[]{:S(2)}, u32[]{:S(2)}) collective-permute-start(bf16[256,128]{1,0:T(8,128)(2,1)S(1)} %get-tuple-element.72), channel_id=1, source_target_pairs={{0,128},{2,130},{4,132},{6,134},{8,136},{10,138},{12,140},{14,142}... | collective-permute-start | bytes 196616 | tf_op jit(solution)/shard_map/ppermute | solution.py:37
  129.3 7.9 %collective-permute-start.28 = (bf16[256,128]{1,0:T(8,128)(2,1)S(1)}, bf16[256,128]{1,0:T(8,128)(2,1)S(1)}, u32[]{:S(2)}, u32[]{:S(2)}) collective-permute-start(bf16[256,128]{1,0:T(8,128)(2,1)S(1)} %get-tuple-element.73), channel_id=1, source_target_pairs={{0,192},{2,194},{4,196},{6,198},{8,200},{10,202},{12,204},{14,206}... | collective-permute-start | bytes 196616 | tf_op jit(solution)/shard_map/ppermute | solution.py:37
  (10 other events, 134.0 us)

commit v4 on v3

--- a/solution.py
+++ b/solution.py
@@ -13,7 +13,7 @@
 CHUNK = 16
 UNROLL = 8
 NEAR, FAR = (0, 1, 2, 4, 7), (3, 5, 6)
-HIGH, LOW = ("zq", "yq", "xq"), ("zp", "yp", "xp", "rep")
+HIGH, LOW = ("zq", "yq", "xq"), ("zp", "yp", "xp")
 ROWS = ("zq", "zp", "yq", "yp", "xq", "xp")
 ALL = ROWS + ("rep",)
 VMEM_LIMIT = 16 * 2**20
@@ -331,10 +331,12 @@
         name="dense",
     )(own, other, features, features_other, masked, masked_other, self_weight, neigh_weight)
 
+    grads_other = lax.ppermute(grads, "rep", swap)
     far = spread_terms(True, rounds, work, counts, back)
-    *far, grads = lax.optimization_barrier((*far, grads))
+    grads = grads + grads_other
     far = [move(far[0], -1, 0, 0), move(far[1], 0, -1, 0), move(far[2], 0, 0, -1)]
     near = spread_terms(False, rounds, work, counts, back)
+    *near, grads = lax.optimization_barrier((*near, grads))
     parts = [near[0], move(near[1], 0, 0, 1), move(near[2], 0, 1, 0), move(near[3], 1, 0, 0)]
     parts.append(move(class_sum([near[4], *far]), -1, -1, -1))
 

time: 139 us -> 138 us (level)
  blocking collectives: 14 us -> 9.36 us
  waiting for transfers between devices: 32.3 us -> 35.5 us
  local copies, waits for them, and re-layouts: 4.29 us -> 6.18 us
  starting transfers between devices: 62.6 us -> 61.1 us
    all_to_all x1, blocking collectives: 14 us -> 9.36 us  [spread(): return lax.all_to_all(copies, axes, 0, 0, tiled=True)]
    all_to_all x1, waiting for transfers between devices: 0.01 us -> 4.4 us  [shards(): cells = jnp.sum(lax.all_to_all(cells, HIGH, 0, 0, tiled=True), axis=0)]
    unnamed x14 -> x20, local copies, waits for them, and re-layouts: 4.25 us -> 6.15 us
    ppermute x26, starting transfers between devices: 56 us -> 54.5 us  [move(): return lax.ppermute(block, ROWS, pairs)]
  transfers between devices with their start and end apart: 30 -> 31, of which waited for: 10 -> 12; matrix products, arithmetic and copies ran while one was open for 3% -> 4% of each run, Pallas kernels for 7% -> 7%
where the time goes in v4:
time: 138 us
  starting transfers between devices  61.1 us (44%)
  waiting for transfers between devices  35.5 us (26%)
  Pallas kernels  18.5 us (13%)
  blocking collectives  9.36 us (7%)
  local copies, waits for them, and re-layouts  6.18 us (4%)
  other arithmetic  5.05 us (4%)
  between operations  2.17 us (2%)
    ppermute x26, starting transfers between devices, move(): return lax.ppermute(block, ROWS, pairs)  54.5 us
    ppermute x26, waiting for transfers between devices, move(): return lax.ppermute(block, ROWS, pairs)  29.7 us
    all_to_all x1, blocking collectives, spread(): return lax.all_to_all(copies, axes, 0, 0, tiled=True)  9.36 us
    pallas_call x2, Pallas kernels, spread_terms(): pl.pallas_call(functools.partial(spread_kernel, far), out_shape=[jax.Shap...  7.89 us
    unnamed x20, local copies, waits for them, and re-layouts  6.15 us
    all_to_all x1, starting transfers between devices, shards(): cells = jnp.sum(lax.all_to_all(cells, HIGH, 0, 0, tiled=True), axis=0)  5.8 us
    pallas_call x2, Pallas kernels, gather_products(): pl.pallas_call(functools.partial(gather_kernel, far), out_shape=jax.Shape...  5.39 us
    all_to_all x1, waiting for transfers between devices, shards(): cells = jnp.sum(lax.all_to_all(cells, HIGH, 0, 0, tiled=True), axis=0)  4.4 us
  transfers between devices with their start and end apart: 31, of which 12 were waited for; matrix products, arithmetic and copies ran while one was open for 4% of the time, Pallas kernels for 7%

profile of v4, /device:TPU:32, one launch (start us, length us, event | category | flops | bytes accessed | tf_op | source)
XLA Modules:
  0.0 137.8 jit_solution(10600132370580477994)
XLA Ops:
  0.6 3.3 %collective-permute-start = (bf16[1,128,128]{2,1,0:T(8,128)(2,1)}, bf16[1,128,128]{2,1,0:T(8,128)(2,1)S(1)}, u32[]{:S(2)}, u32[]{:S(2)}) collective-permute-start(bf16[1,128,128]{2,1,0:T(8,128)(2,1)} %bitcast.5), channel_id=1, source_target_pairs={{0,64},{2,66},{4,68},{6,70},{8,72},{10,74},{12,76},{14,78},{16,80}... | collective-permute-start | bytes 98312 | tf_op jit(solution)/shard_map/ppermute | solution.py:37
  4.0 4.5 %collective-permute-start.1 = (bf16[1,128,128]{2,1,0:T(8,128)(2,1)}, bf16[1,128,128]{2,1,0:T(8,128)(2,1)S(1)}, u32[]{:S(2)}, u32[]{:S(2)}) collective-permute-start(bf16[1,128,128]{2,1,0:T(8,128)(2,1)} %bitcast.6), channel_id=1, source_target_pairs={{0,128},{2,130},{4,132},{6,134},{8,136},{10,138},{12,140},{14,142}... | collective-permute-start | bytes 98312 | tf_op jit(solution)/shard_map/ppermute | solution.py:37
  8.5 2.7 %collective-permute-start.2 = (bf16[1,128,128]{2,1,0:T(8,128)(2,1)}, bf16[1,128,128]{2,1,0:T(8,128)(2,1)S(1)}, u32[]{:S(2)}, u32[]{:S(2)}) collective-permute-start(bf16[1,128,128]{2,1,0:T(8,128)(2,1)} %bitcast.7), channel_id=1, source_target_pairs={{0,192},{2,194},{4,196},{6,198},{8,200},{10,202},{12,204},{14,206}... | collective-permute-start | bytes 98312 | tf_op jit(solution)/shard_map/ppermute | solution.py:37
  16.5 3.1 %collective-permute-start.3 = (bf16[4,128,128]{2,1,0:T(8,128)(2,1)S(1)}, bf16[4,128,128]{2,1,0:T(8,128)(2,1)S(1)}, u32[]{:S(2)}, u32[]{:S(2)}) collective-permute-start(bf16[4,128,128]{2,1,0:T(8,128)(2,1)S(1)} %pad_maximum_fusion), channel_id=1, source_target_pairs={{0,4},{2,6},{4,0},{6,2},{8,12},{10,14},{12,8},{14,10},{16,20},{18,... | collective-permute-start | bytes 393224 | tf_op jit(solution)/shard_map/ppermute | solution.py:37
  19.6 3.2 %collective-permute-start.4 = (bf16[4,128,128]{2,1,0:T(8,128)(2,1)S(1)}, bf16[4,128,128]{2,1,0:T(8,128)(2,1)S(1)}, u32[]{:S(2)}, u32[]{:S(2)}) collective-permute-start(bf16[4,128,128]{2,1,0:T(8,128)(2,1)S(1)} %pad_maximum_fusion), channel_id=1, source_target_pairs={{0,16},{2,18},{4,20},{6,22},{8,24},{10,26},{12,28},{14,30},{16,0},... | collective-permute-start | bytes 393224 | tf_op jit(solution)/shard_map/ppermute | solution.py:37
  23.1 3.5 %collective-permute-done.4 = bf16[4,128,128]{2,1,0:T(8,128)(2,1)S(1)} collective-permute-done((bf16[4,128,128]{2,1,0:T(8,128)(2,1)S(1)}, bf16[4,128,128]{2,1,0:T(8,128)(2,1)S(1)}, u32[]{:S(2)}, u32[]{:S(2)}) %collective-permute-start.4) | collective-permute-done | bytes 131104 | tf_op jit(solution)/shard_map/ppermute | solution.py:37
  26.7 5.0 %collective-permute-done.5 = bf16[4,128,128]{2,1,0:T(8,128)(2,1)S(1)} collective-permute-done((bf16[4,128,128]{2,1,0:T(8,128)(2,1)S(1)}, bf16[4,128,128]{2,1,0:T(8,128)(2,1)S(1)}, u32[]{:S(2)}, u32[]{:S(2)}) %collective-permute-start.5) | collective-permute-done | bytes 131104 | tf_op jit(solution)/shard_map/ppermute | solution.py:37
  37.8 3.4 %copy-done = s32[128,128,128]{2,1,0:T(8,128)S(1)} copy-done((s32[128,128,128]{2,1,0:T(8,128)S(1)}, s32[128,128,128]{2,1,0:T(8,128)}, u32[]{:S(2)}) %copy-start) | copy-done | bytes 8388632
  41.6 3.9 %collective-permute-done.6.refs_4_ = bf16[16,128,128]{2,1,0:T(8,128)(2,1)S(1)} collective-permute-done((bf16[16,128,128]{2,1,0:T(8,128)(2,1)S(1)}, bf16[16,128,128]{2,1,0:T(8,128)(2,1)S(1)}, u32[]{:S(2)}, u32[]{:S(2)}) %collective-permute-start.6) | collective-permute-done | bytes 524320 | tf_op jit(solution)/shard_map/ppermute | solution.py:37
  51.3 3.1 %near_products.1.refs_3_ = f32[2,128,128]{2,1,0:T(8,128)S(1)} custom-call(s32[2]{0:T(128)S(1)} %pad_add_fusion.rounds_ref, s32[144]{0:T(256)S(1)} %broadcast_add_fusion.work_ref, s8[128,128,128]{2,1,0:T(32,128)(4,1)S(1)} %cast_counts.1.counts_ref, bf16[16,128,128]{2,1,0:T(8,128)(2,1)S(1)} %constant_dynamic-update-slice_fusion.refs_0_, ...), custom_call_target="tpu_custom_call" | custom-call | flops 536870912 | bytes 4194304 | tf_op jit(solution)/shard_map/near_products/pallas_call | solution.py:109
  62.7 3.5 %far_terms.1 = (bf16[16,128,128]{2,1,0:T(8,128)(2,1)S(1)}, bf16[16,128,128]{2,1,0:T(8,128)(2,1)}, bf16[16,128,128]{2,1,0:T(8,128)(2,1)}) custom-call(s32[2]{0:T(128)S(1)} %pad_add_fusion.rounds_ref, s32[144]{0:T(256)S(1)} %broadcast_add_fusion.work_ref, s8[128,128,128]{2,1,0:T(32,128)(4,1)S(1)} %cast_counts.1.counts_ref, ...), custom_call_target="tpu_custom_call" | custom-call | flops 536870912 | bytes 4194304 | tf_op jit(solution)/shard_map/far_terms/pallas_call | solution.py:177
  68.1 2.7 %collective-permute-start.22 = (bf16[16,128,128]{2,1,0:T(8,128)(2,1)}, bf16[16,128,128]{2,1,0:T(8,128)(2,1)}, u32[]{:S(2)}, u32[]{:S(2)}) collective-permute-start(bf16[16,128,128]{2,1,0:T(8,128)(2,1)} %get-tuple-element.69), channel_id=1, source_target_pairs={{0,6},{2,0},{4,2},{6,4},{8,14},{10,8},{12,10},{14,12},{16,22},{18,... | collective-permute-start | bytes 1572872 | tf_op jit(solution)/shard_map/ppermute | solution.py:37
  70.9 4.4 %near_terms.1 = (bf16[16,128,128]{2,1,0:T(8,128)(2,1)S(1)}, bf16[16,128,128]{2,1,0:T(8,128)(2,1)}, bf16[16,128,128]{2,1,0:T(8,128)(2,1)}, bf16[16,128,128]{2,1,0:T(8,128)(2,1)S(1)}, bf16[16,128,128]{2,1,0:T(8,128)(2,1)S(1)}) custom-call(s32[2]{0:T(128)S(1)} %pad_add_fusion.rounds_ref, s32[144]{0:T(256)S(1)} %broadcast_add_fusion.work_ref, ...), custom_call_target="tpu_custom_call" | custom-call | flops 536870912 | bytes 4194304 | tf_op jit(solution)/shard_map/near_terms/pallas_call | solution.py:177
  76.9 5.8 %all-to-all-start = ((f32[16,32,128]{2,1,0:T(8,128)}), f32[16,32,128]{2,1,0:T(8,128)S(1)}, u32[]{:S(2)}, u32[]{:S(2)}) async-start(f32[16,32,128]{2,1,0:T(8,128)} %bitcast.3), calls=%async_computation | async-start | bytes 524288 | tf_op jit(solution)/shard_map/all_to_all | solution.py:344
  89.4 4.2 %collective-permute-start.23 = (bf16[16,128,128]{2,1,0:T(8,128)(2,1)}, bf16[16,128,128]{2,1,0:T(8,128)(2,1)S(1)}, u32[]{:S(2)}, u32[]{:S(2)}) collective-permute-start(bf16[16,128,128]{2,1,0:T(8,128)(2,1)} %class_sum.1), channel_id=1, source_target_pairs={{0,254},{2,248},{4,250},{6,252},{8,230},{10,224},{12,226},{14,228}... | collective-permute-start | bytes 1572872 | tf_op jit(solution)/shard_map/ppermute | solution.py:37
  93.7 4.4 %all-to-all-done = f32[16,32,128]{2,1,0:T(8,128)S(1)} async-done(((f32[16,32,128]{2,1,0:T(8,128)}), f32[16,32,128]{2,1,0:T(8,128)S(1)}, u32[]{:S(2)}, u32[]{:S(2)}) %all-to-all-start) | async-done | bytes 262176 | tf_op jit(solution)/shard_map/all_to_all | solution.py:344
  98.1 9.4 %all_to_all.10 = f32[8,32,128]{2,1,0:T(8,128)S(1)} all-to-all(f32[8,32,128]{2,1,0:T(8,128)S(1)} %broadcast_in_dim.148), channel_id=1, replica_groups=mesh['zq'=4,'zp'=2,'yq'=2,'yp'=2,'xq'=2,'xp'=2,'rep'=2] {'zp','yp','xp'}, dimensions={0} | all-to-all | bytes 262144 | tf_op jit(solution)/shard_map/all_to_all | solution.py:45
  107.9 2.6 %collective-permute-start.24 = (bf16[544,128]{1,0:T(8,128)(2,1)S(1)}, bf16[544,128]{1,0:T(8,128)(2,1)S(1)}, u32[]{:S(2)}, u32[]{:S(2)}) collective-permute-start(bf16[544,128]{1,0:T(8,128)(2,1)S(1)} %get-tuple-element.71), channel_id=1, source_target_pairs={{0,4},{2,6},{4,0},{6,2},{8,12},{10,14},{12,8},{14,10},{16,20},{18,... | collective-permute-start | bytes 417800 | tf_op jit(solution)/shard_map/ppermute | solution.py:37
  110.5 3.3 %collective-permute-start.25 = (bf16[544,128]{1,0:T(8,128)(2,1)S(1)}, bf16[544,128]{1,0:T(8,128)(2,1)S(1)}, u32[]{:S(2)}, u32[]{:S(2)}) collective-permute-start(bf16[544,128]{1,0:T(8,128)(2,1)S(1)} %get-tuple-element.72), channel_id=1, source_target_pairs={{0,16},{2,18},{4,20},{6,22},{8,24},{10,26},{12,28},{14,30},{16,0},... | collective-permute-start | bytes 417800 | tf_op jit(solution)/shard_map/ppermute | solution.py:37
  115.0 4.6 %collective-permute-done.25.refs_2_ = bf16[544,128]{1,0:T(8,128)(2,1)S(1)} collective-permute-done((bf16[544,128]{1,0:T(8,128)(2,1)S(1)}, bf16[544,128]{1,0:T(8,128)(2,1)S(1)}, u32[]{:S(2)}, u32[]{:S(2)}) %collective-permute-start.25) | collective-permute-done | bytes 139296 | tf_op jit(solution)/shard_map/ppermute | solution.py:37
  119.6 3.1 %collective-permute-done.26.refs_3_ = bf16[544,128]{1,0:T(8,128)(2,1)S(1)} collective-permute-done((bf16[544,128]{1,0:T(8,128)(2,1)S(1)}, bf16[544,128]{1,0:T(8,128)(2,1)S(1)}, u32[]{:S(2)}, u32[]{:S(2)}) %collective-permute-start.26) | collective-permute-done | bytes 139296 | tf_op jit(solution)/shard_map/ppermute | solution.py:37
  122.8 4.5 %collective-permute-start.27 = (bf16[256,128]{1,0:T(8,128)(2,1)S(1)}, bf16[256,128]{1,0:T(8,128)(2,1)S(1)}, u32[]{:S(2)}, u32[]{:S(2)}) collective-permute-start(bf16[256,128]{1,0:T(8,128)(2,1)S(1)} %get-tuple-element.75), channel_id=1, source_target_pairs={{0,64},{2,66},{4,68},{6,70},{8,72},{10,74},{12,76},{14,78},{16,80}... | collective-permute-start | bytes 196616 | tf_op jit(solution)/shard_map/ppermute | solution.py:37
  128.2 2.7 %collective-permute-start.29 = (bf16[256,128]{1,0:T(8,128)(2,1)S(1)}, bf16[256,128]{1,0:T(8,128)(2,1)S(1)}, u32[]{:S(2)}, u32[]{:S(2)}) collective-permute-start(bf16[256,128]{1,0:T(8,128)(2,1)S(1)} %get-tuple-element.77), channel_id=1, source_target_pairs={{0,192},{2,194},{4,196},{6,198},{8,200},{10,202},{12,204},{14,206}... | collective-permute-start | bytes 196616 | tf_op jit(solution)/shard_map/ppermute | solution.py:37
  130.9 5.6 %collective-permute-done.28.refs_2_ = bf16[256,128]{1,0:T(8,128)(2,1)S(1)} collective-permute-done((bf16[256,128]{1,0:T(8,128)(2,1)S(1)}, bf16[256,128]{1,0:T(8,128)(2,1)S(1)}, u32[]{:S(2)}, u32[]{:S(2)}) %collective-permute-start.28) | collective-permute-done | bytes 65568 | tf_op jit(solution)/shard_map/ppermute | solution.py:37
  (86 shorter events, 39.2 us)
Async XLA Ops:
  0.6 15.0 %collective-permute-start = (bf16[1,128,128]{2,1,0:T(8,128)(2,1)}, bf16[1,128,128]{2,1,0:T(8,128)(2,1)S(1)}, u32[]{:S(2)}, u32[]{:S(2)}) collective-permute-start(bf16[1,128,128]{2,1,0:T(8,128)(2,1)} %bitcast.5), channel_id=1, source_target_pairs={{0,64},{2,66},{4,68},{6,70},{8,72},{10,74},{12,76},{14,78},{16,80}... | collective-permute-start | bytes 98312 | tf_op jit(solution)/shard_map/ppermute | solution.py:37
  4.0 11.7 %collective-permute-start.1 = (bf16[1,128,128]{2,1,0:T(8,128)(2,1)}, bf16[1,128,128]{2,1,0:T(8,128)(2,1)S(1)}, u32[]{:S(2)}, u32[]{:S(2)}) collective-permute-start(bf16[1,128,128]{2,1,0:T(8,128)(2,1)} %bitcast.6), channel_id=1, source_target_pairs={{0,128},{2,130},{4,132},{6,134},{8,136},{10,138},{12,140},{14,142}... | collective-permute-start | bytes 98312 | tf_op jit(solution)/shard_map/ppermute | solution.py:37
  8.5 7.2 %collective-permute-start.2 = (bf16[1,128,128]{2,1,0:T(8,128)(2,1)}, bf16[1,128,128]{2,1,0:T(8,128)(2,1)S(1)}, u32[]{:S(2)}, u32[]{:S(2)}) collective-permute-start(bf16[1,128,128]{2,1,0:T(8,128)(2,1)} %bitcast.7), channel_id=1, source_target_pairs={{0,192},{2,194},{4,196},{6,198},{8,200},{10,202},{12,204},{14,206}... | collective-permute-start | bytes 98312 | tf_op jit(solution)/shard_map/ppermute | solution.py:37
  22.8 8.9 %collective-permute-start.5 = (bf16[4,128,128]{2,1,0:T(8,128)(2,1)S(1)}, bf16[4,128,128]{2,1,0:T(8,128)(2,1)S(1)}, u32[]{:S(2)}, u32[]{:S(2)}) collective-permute-start(bf16[4,128,128]{2,1,0:T(8,128)(2,1)S(1)} %pad_maximum_fusion), channel_id=1, source_target_pairs={{0,20},{2,22},{4,16},{6,18},{8,28},{10,30},{12,24},{14,26},{16,4},... | collective-permute-start | bytes 393224 | tf_op jit(solution)/shard_map/ppermute | solution.py:37
  31.7 13.8 %collective-permute-start.6 = (bf16[16,128,128]{2,1,0:T(8,128)(2,1)S(1)}, bf16[16,128,128]{2,1,0:T(8,128)(2,1)S(1)}, u32[]{:S(2)}, u32[]{:S(2)}) collective-permute-start(bf16[16,128,128]{2,1,0:T(8,128)(2,1)S(1)} %constant_dynamic-update-slice_fusion.refs_0_), channel_id=1, source_target_pairs={{0,254},{2,248},{4,250},{6,252},{8,230},{10,224},{12,226},{14,228}... | collective-permute-start | bytes 1572872 | tf_op jit(solution)/shard_map/ppermute | solution.py:37
  33.8 14.9 %collective-permute-start.10 = (bf16[16,128,128]{2,1,0:T(8,128)(2,1)S(1)}, bf16[16,128,128]{2,1,0:T(8,128)(2,1)S(1)}, u32[]{:S(2)}, u32[]{:S(2)}) collective-permute-start(bf16[16,128,128]{2,1,0:T(8,128)(2,1)S(1)} %constant_dynamic-update-slice_fusion.refs_0_), channel_id=1, source_target_pairs={{0,2},{2,4},{4,6},{6,0},{8,10},{10,12},{12,14},{14,8},{16,18},{18,... | collective-permute-start | bytes 1572872 | tf_op jit(solution)/shard_map/ppermute | solution.py:37
  35.6 15.1 %collective-permute-start.11 = (bf16[16,128,128]{2,1,0:T(8,128)(2,1)S(1)}, bf16[16,128,128]{2,1,0:T(8,128)(2,1)S(1)}, u32[]{:S(2)}, u32[]{:S(2)}) collective-permute-start(bf16[16,128,128]{2,1,0:T(8,128)(2,1)S(1)} %constant_dynamic-update-slice_fusion.refs_0_), channel_id=1, source_target_pairs={{0,8},{2,10},{4,12},{6,14},{8,16},{10,18},{12,20},{14,22},{16,24},... | collective-permute-start | bytes 1572872 | tf_op jit(solution)/shard_map/ppermute | solution.py:37
  36.7 14.1 %collective-permute-start.12 = (bf16[16,128,128]{2,1,0:T(8,128)(2,1)S(1)}, bf16[16,128,128]{2,1,0:T(8,128)(2,1)S(1)}, u32[]{:S(2)}, u32[]{:S(2)}) collective-permute-start(bf16[16,128,128]{2,1,0:T(8,128)(2,1)S(1)} %constant_dynamic-update-slice_fusion.refs_0_), channel_id=1, source_target_pairs={{0,32},{2,34},{4,36},{6,38},{8,40},{10,42},{12,44},{14,46},{16,48}... | collective-permute-start | bytes 1572872 | tf_op jit(solution)/shard_map/ppermute | solution.py:37
  45.5 9.8 %collective-permute-start.7 = (bf16[16,128,128]{2,1,0:T(8,128)(2,1)S(1)}, bf16[16,128,128]{2,1,0:T(8,128)(2,1)S(1)}, u32[]{:S(2)}, u32[]{:S(2)}) collective-permute-start(bf16[16,128,128]{2,1,0:T(8,128)(2,1)S(1)} %collective-permute-done.6.refs_4_), channel_id=1, source_target_pairs={{0,224},{2,226},{4,228},{6,230},{8,232},{10,234},{12,236},{14,238}... | collective-permute-start | bytes 1572872 | tf_op jit(solution)/shard_map/ppermute | solution.py:37
  46.5 9.7 %collective-permute-start.8 = (bf16[16,128,128]{2,1,0:T(8,128)(2,1)S(1)}, bf16[16,128,128]{2,1,0:T(8,128)(2,1)S(1)}, u32[]{:S(2)}, u32[]{:S(2)}) collective-permute-start(bf16[16,128,128]{2,1,0:T(8,128)(2,1)S(1)} %collective-permute-done.6.refs_4_), channel_id=1, source_target_pairs={{0,24},{2,26},{4,28},{6,30},{8,0},{10,2},{12,4},{14,6},{16,8},{18,... | collective-permute-start | bytes 1572872 | tf_op jit(solution)/shard_map/ppermute | solution.py:37
  48.7 9.2 %collective-permute-start.9 = (bf16[16,128,128]{2,1,0:T(8,128)(2,1)S(1)}, bf16[16,128,128]{2,1,0:T(8,128)(2,1)S(1)}, u32[]{:S(2)}, u32[]{:S(2)}) collective-permute-start(bf16[16,128,128]{2,1,0:T(8,128)(2,1)S(1)} %collective-permute-done.6.refs_4_), channel_id=1, source_target_pairs={{0,6},{2,0},{4,2},{6,4},{8,14},{10,8},{12,10},{14,12},{16,22},{18,... | collective-permute-start | bytes 1572872 | tf_op jit(solution)/shard_map/ppermute | solution.py:37
  66.1 18.0 %collective-permute-start.20 = (bf16[16,128,128]{2,1,0:T(8,128)(2,1)S(1)}, bf16[16,128,128]{2,1,0:T(8,128)(2,1)S(1)}, u32[]{:S(2)}, u32[]{:S(2)}) collective-permute-start(bf16[16,128,128]{2,1,0:T(8,128)(2,1)S(1)} %get-tuple-element.67), channel_id=1, source_target_pairs={{0,224},{2,226},{4,228},{6,230},{8,232},{10,234},{12,236},{14,238}... | collective-permute-start | bytes 1572872 | tf_op jit(solution)/shard_map/ppermute | solution.py:37
  67.6 18.6 %collective-permute-start.21 = (bf16[16,128,128]{2,1,0:T(8,128)(2,1)}, bf16[16,128,128]{2,1,0:T(8,128)(2,1)S(1)}, u32[]{:S(2)}, u32[]{:S(2)}) collective-permute-start(bf16[16,128,128]{2,1,0:T(8,128)(2,1)} %get-tuple-element.68), channel_id=1, source_target_pairs={{0,24},{2,26},{4,28},{6,30},{8,0},{10,2},{12,4},{14,6},{16,8},{18,... | collective-permute-start | bytes 1572872 | tf_op jit(solution)/shard_map/ppermute | solution.py:37
  68.1 18.1 %collective-permute-start.22 = (bf16[16,128,128]{2,1,0:T(8,128)(2,1)}, bf16[16,128,128]{2,1,0:T(8,128)(2,1)}, u32[]{:S(2)}, u32[]{:S(2)}) collective-permute-start(bf16[16,128,128]{2,1,0:T(8,128)(2,1)} %get-tuple-element.69), channel_id=1, source_target_pairs={{0,6},{2,0},{4,2},{6,4},{8,14},{10,8},{12,10},{14,12},{16,22},{18,... | collective-permute-start | bytes 1572872 | tf_op jit(solution)/shard_map/ppermute | solution.py:37
  76.9 21.1 %all-to-all-start = ((f32[16,32,128]{2,1,0:T(8,128)}), f32[16,32,128]{2,1,0:T(8,128)S(1)}, u32[]{:S(2)}, u32[]{:S(2)}) async-start(f32[16,32,128]{2,1,0:T(8,128)} %bitcast.3), calls=%async_computation | async-start | bytes 524288 | tf_op jit(solution)/shard_map/all_to_all | solution.py:344
  82.8 24.7 %collective-permute-start.17 = (bf16[16,128,128]{2,1,0:T(8,128)(2,1)}, bf16[16,128,128]{2,1,0:T(8,128)(2,1)S(1)}, u32[]{:S(2)}, u32[]{:S(2)}) collective-permute-start(bf16[16,128,128]{2,1,0:T(8,128)(2,1)} %get-tuple-element.63), channel_id=1, source_target_pairs={{0,2},{2,4},{4,6},{6,0},{8,10},{10,12},{12,14},{14,8},{16,18},{18,... | collective-permute-start | bytes 1572872 | tf_op jit(solution)/shard_map/ppermute | solution.py:37
  83.1 24.4 %collective-permute-start.18 = (bf16[16,128,128]{2,1,0:T(8,128)(2,1)}, bf16[16,128,128]{2,1,0:T(8,128)(2,1)S(1)}, u32[]{:S(2)}, u32[]{:S(2)}) collective-permute-start(bf16[16,128,128]{2,1,0:T(8,128)(2,1)} %get-tuple-element.64), channel_id=1, source_target_pairs={{0,8},{2,10},{4,12},{6,14},{8,16},{10,18},{12,20},{14,22},{16,24},... | collective-permute-start | bytes 1572872 | tf_op jit(solution)/shard_map/ppermute | solution.py:37
  84.1 23.4 %collective-permute-start.19 = (bf16[16,128,128]{2,1,0:T(8,128)(2,1)}, bf16[16,128,128]{2,1,0:T(8,128)(2,1)S(1)}, u32[]{:S(2)}, u32[]{:S(2)}) collective-permute-start(bf16[16,128,128]{2,1,0:T(8,128)(2,1)} %copy-done.6), channel_id=1, source_target_pairs={{0,32},{2,34},{4,36},{6,38},{8,40},{10,42},{12,44},{14,46},{16,48}... | collective-permute-start | bytes 1572872 | tf_op jit(solution)/shard_map/ppermute | solution.py:37
  89.4 18.1 %collective-permute-start.23 = (bf16[16,128,128]{2,1,0:T(8,128)(2,1)}, bf16[16,128,128]{2,1,0:T(8,128)(2,1)S(1)}, u32[]{:S(2)}, u32[]{:S(2)}) collective-permute-start(bf16[16,128,128]{2,1,0:T(8,128)(2,1)} %class_sum.1), channel_id=1, source_target_pairs={{0,254},{2,248},{4,250},{6,252},{8,230},{10,224},{12,226},{14,228}... | collective-permute-start | bytes 1572872 | tf_op jit(solution)/shard_map/ppermute | solution.py:37
  110.5 9.2 %collective-permute-start.25 = (bf16[544,128]{1,0:T(8,128)(2,1)S(1)}, bf16[544,128]{1,0:T(8,128)(2,1)S(1)}, u32[]{:S(2)}, u32[]{:S(2)}) collective-permute-start(bf16[544,128]{1,0:T(8,128)(2,1)S(1)} %get-tuple-element.72), channel_id=1, source_target_pairs={{0,16},{2,18},{4,20},{6,22},{8,24},{10,26},{12,28},{14,30},{16,0},... | collective-permute-start | bytes 417800 | tf_op jit(solution)/shard_map/ppermute | solution.py:37
  113.8 9.0 %collective-permute-start.26 = (bf16[544,128]{1,0:T(8,128)(2,1)S(1)}, bf16[544,128]{1,0:T(8,128)(2,1)S(1)}, u32[]{:S(2)}, u32[]{:S(2)}) collective-permute-start(bf16[544,128]{1,0:T(8,128)(2,1)S(1)} %get-tuple-element.73), channel_id=1, source_target_pairs={{0,20},{2,22},{4,16},{6,18},{8,28},{10,30},{12,24},{14,26},{16,4},... | collective-permute-start | bytes 417800 | tf_op jit(solution)/shard_map/ppermute | solution.py:37
  122.8 8.1 %collective-permute-start.27 = (bf16[256,128]{1,0:T(8,128)(2,1)S(1)}, bf16[256,128]{1,0:T(8,128)(2,1)S(1)}, u32[]{:S(2)}, u32[]{:S(2)}) collective-permute-start(bf16[256,128]{1,0:T(8,128)(2,1)S(1)} %get-tuple-element.75), channel_id=1, source_target_pairs={{0,64},{2,66},{4,68},{6,70},{8,72},{10,74},{12,76},{14,78},{16,80}... | collective-permute-start | bytes 196616 | tf_op jit(solution)/shard_map/ppermute | solution.py:37
  127.3 9.2 %collective-permute-start.28 = (bf16[256,128]{1,0:T(8,128)(2,1)S(1)}, bf16[256,128]{1,0:T(8,128)(2,1)S(1)}, u32[]{:S(2)}, u32[]{:S(2)}) collective-permute-start(bf16[256,128]{1,0:T(8,128)(2,1)S(1)} %get-tuple-element.76), channel_id=1, source_target_pairs={{0,128},{2,130},{4,132},{6,134},{8,136},{10,138},{12,140},{14,142}... | collective-permute-start | bytes 196616 | tf_op jit(solution)/shard_map/ppermute | solution.py:37
  128.2 8.3 %collective-permute-start.29 = (bf16[256,128]{1,0:T(8,128)(2,1)S(1)}, bf16[256,128]{1,0:T(8,128)(2,1)S(1)}, u32[]{:S(2)}, u32[]{:S(2)}) collective-permute-start(bf16[256,128]{1,0:T(8,128)(2,1)S(1)} %get-tuple-element.77), channel_id=1, source_target_pairs={{0,192},{2,194},{4,196},{6,198},{8,200},{10,202},{12,204},{14,206}... | collective-permute-start | bytes 196616 | tf_op jit(solution)/shard_map/ppermute | solution.py:37
  (14 other events, 132.3 us)

commit v5 on v4

--- a/solution.py
+++ b/solution.py
@@ -194,17 +194,19 @@
 
 
 def class_kernel(*refs):
-    @pl.loop(0, refs[0].shape[0])
-    def _(k):
+    for k in range(refs[0].shape[0]):
         refs[-1][k] = add_up(refs[:-1], k).astype(bf16)
 
 
 def class_sum(parts):
+    count, rows, columns = parts[0].shape
+    spec = pl.BlockSpec((count // 4, rows, columns), lambda i: (i, 0, 0))
     return pl.pallas_call(
         class_kernel,
         out_shape=jax.ShapeDtypeStruct(parts[0].shape, bf16),
-        in_specs=[VMEM] * len(parts),
-        out_specs=VMEM,
+        grid=(4,),
+        in_specs=[spec] * len(parts),
+        out_specs=spec,
         compiler_params=params(),
         name="class_sum",
     )(*parts)

time: 138 us -> 139 us (level)
  transfers between devices with their start and end apart: 31 -> 31, of which waited for: 12 -> 12; matrix products, arithmetic and copies ran while one was open for 4% -> 4% of each run, Pallas kernels for 7% -> 8%
where the time goes in v5:
time: 139 us
  starting transfers between devices  61.1 us (44%)
  waiting for transfers between devices  34.4 us (25%)
  Pallas kernels  19.5 us (14%)
  blocking collectives  10.2 us (7%)
  local copies, waits for them, and re-layouts  6.18 us (4%)
  other arithmetic  5.05 us (4%)
  between operations  2.17 us (2%)
    ppermute x26, starting transfers between devices, move(): return lax.ppermute(block, ROWS, pairs)  55 us
    ppermute x26, waiting for transfers between devices, move(): return lax.ppermute(block, ROWS, pairs)  29.6 us
    all_to_all x1, blocking collectives, spread(): return lax.all_to_all(copies, axes, 0, 0, tiled=True)  10.2 us
    pallas_call x2, Pallas kernels, spread_terms(): pl.pallas_call(functools.partial(spread_kernel, far), out_shape=[jax.Shap...  7.88 us
    unnamed x20, local copies, waits for them, and re-layouts  6.15 us
    pallas_call x2, Pallas kernels, gather_products(): pl.pallas_call(functools.partial(gather_kernel, far), out_shape=jax.Shape...  5.36 us
    all_to_all x1, starting transfers between devices, shards(): cells = jnp.sum(lax.all_to_all(cells, HIGH, 0, 0, tiled=True), axis=0)  5.31 us
    all_to_all x1, waiting for transfers between devices, shards(): cells = jnp.sum(lax.all_to_all(cells, HIGH, 0, 0, tiled=True), axis=0)  3.45 us
  transfers between devices with their start and end apart: 31, of which 12 were waited for; matrix products, arithmetic and copies ran while one was open for 4% of the time, Pallas kernels for 8%

profile of v5, /device:TPU:32, one launch (start us, length us, event | category | flops | bytes accessed | tf_op | source)
XLA Modules:
  0.0 138.6 jit_solution(15687276925977724296)
XLA Ops:
  0.6 3.3 %collective-permute-start = (bf16[1,128,128]{2,1,0:T(8,128)(2,1)}, bf16[1,128,128]{2,1,0:T(8,128)(2,1)S(1)}, u32[]{:S(2)}, u32[]{:S(2)}) collective-permute-start(bf16[1,128,128]{2,1,0:T(8,128)(2,1)} %bitcast.5), channel_id=1, source_target_pairs={{0,64},{2,66},{4,68},{6,70},{8,72},{10,74},{12,76},{14,78},{16,80}... | collective-permute-start | bytes 98312 | tf_op jit(solution)/shard_map/ppermute | solution.py:37
  4.0 4.5 %collective-permute-start.1 = (bf16[1,128,128]{2,1,0:T(8,128)(2,1)}, bf16[1,128,128]{2,1,0:T(8,128)(2,1)S(1)}, u32[]{:S(2)}, u32[]{:S(2)}) collective-permute-start(bf16[1,128,128]{2,1,0:T(8,128)(2,1)} %bitcast.6), channel_id=1, source_target_pairs={{0,128},{2,130},{4,132},{6,134},{8,136},{10,138},{12,140},{14,142}... | collective-permute-start | bytes 98312 | tf_op jit(solution)/shard_map/ppermute | solution.py:37
  8.5 2.7 %collective-permute-start.2 = (bf16[1,128,128]{2,1,0:T(8,128)(2,1)}, bf16[1,128,128]{2,1,0:T(8,128)(2,1)S(1)}, u32[]{:S(2)}, u32[]{:S(2)}) collective-permute-start(bf16[1,128,128]{2,1,0:T(8,128)(2,1)} %bitcast.7), channel_id=1, source_target_pairs={{0,192},{2,194},{4,196},{6,198},{8,200},{10,202},{12,204},{14,206}... | collective-permute-start | bytes 98312 | tf_op jit(solution)/shard_map/ppermute | solution.py:37
  16.5 3.1 %collective-permute-start.3 = (bf16[4,128,128]{2,1,0:T(8,128)(2,1)S(1)}, bf16[4,128,128]{2,1,0:T(8,128)(2,1)S(1)}, u32[]{:S(2)}, u32[]{:S(2)}) collective-permute-start(bf16[4,128,128]{2,1,0:T(8,128)(2,1)S(1)} %pad_maximum_fusion), channel_id=1, source_target_pairs={{0,4},{2,6},{4,0},{6,2},{8,12},{10,14},{12,8},{14,10},{16,20},{18,... | collective-permute-start | bytes 393224 | tf_op jit(solution)/shard_map/ppermute | solution.py:37
  19.6 3.2 %collective-permute-start.4 = (bf16[4,128,128]{2,1,0:T(8,128)(2,1)S(1)}, bf16[4,128,128]{2,1,0:T(8,128)(2,1)S(1)}, u32[]{:S(2)}, u32[]{:S(2)}) collective-permute-start(bf16[4,128,128]{2,1,0:T(8,128)(2,1)S(1)} %pad_maximum_fusion), channel_id=1, source_target_pairs={{0,16},{2,18},{4,20},{6,22},{8,24},{10,26},{12,28},{14,30},{16,0},... | collective-permute-start | bytes 393224 | tf_op jit(solution)/shard_map/ppermute | solution.py:37
  23.1 3.5 %collective-permute-done.4 = bf16[4,128,128]{2,1,0:T(8,128)(2,1)S(1)} collective-permute-done((bf16[4,128,128]{2,1,0:T(8,128)(2,1)S(1)}, bf16[4,128,128]{2,1,0:T(8,128)(2,1)S(1)}, u32[]{:S(2)}, u32[]{:S(2)}) %collective-permute-start.4) | collective-permute-done | bytes 131104 | tf_op jit(solution)/shard_map/ppermute | solution.py:37
  26.7 5.0 %collective-permute-done.5 = bf16[4,128,128]{2,1,0:T(8,128)(2,1)S(1)} collective-permute-done((bf16[4,128,128]{2,1,0:T(8,128)(2,1)S(1)}, bf16[4,128,128]{2,1,0:T(8,128)(2,1)S(1)}, u32[]{:S(2)}, u32[]{:S(2)}) %collective-permute-start.5) | collective-permute-done | bytes 131104 | tf_op jit(solution)/shard_map/ppermute | solution.py:37
  37.8 3.4 %copy-done = s32[128,128,128]{2,1,0:T(8,128)S(1)} copy-done((s32[128,128,128]{2,1,0:T(8,128)S(1)}, s32[128,128,128]{2,1,0:T(8,128)}, u32[]{:S(2)}) %copy-start) | copy-done | bytes 8388632
  41.6 3.9 %collective-permute-done.6.refs_4_ = bf16[16,128,128]{2,1,0:T(8,128)(2,1)S(1)} collective-permute-done((bf16[16,128,128]{2,1,0:T(8,128)(2,1)S(1)}, bf16[16,128,128]{2,1,0:T(8,128)(2,1)S(1)}, u32[]{:S(2)}, u32[]{:S(2)}) %collective-permute-start.6) | collective-permute-done | bytes 524320 | tf_op jit(solution)/shard_map/ppermute | solution.py:37
  51.3 3.3 %near_products.1.refs_3_ = f32[2,128,128]{2,1,0:T(8,128)S(1)} custom-call(s32[2]{0:T(128)S(1)} %pad_add_fusion.rounds_ref, s32[144]{0:T(256)S(1)} %broadcast_add_fusion.work_ref, s8[128,128,128]{2,1,0:T(32,128)(4,1)S(1)} %cast_counts.1.counts_ref, bf16[16,128,128]{2,1,0:T(8,128)(2,1)S(1)} %constant_dynamic-update-slice_fusion.refs_0_, ...), custom_call_target="tpu_custom_call" | custom-call | flops 536870912 | bytes 4194304 | tf_op jit(solution)/shard_map/near_products/pallas_call | solution.py:109
  62.4 3.2 %far_terms.1 = (bf16[16,128,128]{2,1,0:T(8,128)(2,1)S(1)}, bf16[16,128,128]{2,1,0:T(8,128)(2,1)}, bf16[16,128,128]{2,1,0:T(8,128)(2,1)}) custom-call(s32[2]{0:T(128)S(1)} %pad_add_fusion.rounds_ref, s32[144]{0:T(256)S(1)} %broadcast_add_fusion.work_ref, s8[128,128,128]{2,1,0:T(32,128)(4,1)S(1)} %cast_counts.1.counts_ref, ...), custom_call_target="tpu_custom_call" | custom-call | flops 536870912 | bytes 4194304 | tf_op jit(solution)/shard_map/far_terms/pallas_call | solution.py:177
  70.9 4.6 %near_terms.1 = (bf16[16,128,128]{2,1,0:T(8,128)(2,1)S(1)}, bf16[16,128,128]{2,1,0:T(8,128)(2,1)}, bf16[16,128,128]{2,1,0:T(8,128)(2,1)}, bf16[16,128,128]{2,1,0:T(8,128)(2,1)S(1)}, bf16[16,128,128]{2,1,0:T(8,128)(2,1)S(1)}) custom-call(s32[2]{0:T(128)S(1)} %pad_add_fusion.rounds_ref, s32[144]{0:T(256)S(1)} %broadcast_add_fusion.work_ref, ...), custom_call_target="tpu_custom_call" | custom-call | flops 536870912 | bytes 4194304 | tf_op jit(solution)/shard_map/near_terms/pallas_call | solution.py:177
  77.2 5.3 %all-to-all-start = ((f32[16,32,128]{2,1,0:T(8,128)}), f32[16,32,128]{2,1,0:T(8,128)S(1)}, u32[]{:S(2)}, u32[]{:S(2)}) async-start(f32[16,32,128]{2,1,0:T(8,128)} %bitcast.3), calls=%async_computation | async-start | bytes 524288 | tf_op jit(solution)/shard_map/all_to_all | solution.py:346
  87.0 3.3 %class_sum.1 = bf16[16,128,128]{2,1,0:T(8,128)(2,1)} custom-call(bf16[16,128,128]{2,1,0:T(8,128)(2,1)S(1)} %copy-done.2, bf16[16,128,128]{2,1,0:T(8,128)(2,1)S(1)} %collective-permute-done.20.refs_1_, bf16[16,128,128]{2,1,0:T(8,128)(2,1)S(1)} %collective-permute-done.21.refs_2_, bf16[16,128,128]{2,1,0:T(8,128)(2,1)} %collective-permute-done.22.refs_3_), custom_call_target="tpu_custom_call" | custom-call | tf_op jit(solution)/shard_map/class_sum/pallas_call | solution.py:204
  90.2 4.1 %collective-permute-start.23 = (bf16[16,128,128]{2,1,0:T(8,128)(2,1)}, bf16[16,128,128]{2,1,0:T(8,128)(2,1)S(1)}, u32[]{:S(2)}, u32[]{:S(2)}) collective-permute-start(bf16[16,128,128]{2,1,0:T(8,128)(2,1)} %class_sum.1), channel_id=1, source_target_pairs={{0,254},{2,248},{4,250},{6,252},{8,230},{10,224},{12,226},{14,228}... | collective-permute-start | bytes 1572872 | tf_op jit(solution)/shard_map/ppermute | solution.py:37
  94.3 3.5 %all-to-all-done = f32[16,32,128]{2,1,0:T(8,128)S(1)} async-done(((f32[16,32,128]{2,1,0:T(8,128)}), f32[16,32,128]{2,1,0:T(8,128)S(1)}, u32[]{:S(2)}, u32[]{:S(2)}) %all-to-all-start) | async-done | bytes 262176 | tf_op jit(solution)/shard_map/all_to_all | solution.py:346
  97.8 10.2 %all_to_all.10 = f32[8,32,128]{2,1,0:T(8,128)S(1)} all-to-all(f32[8,32,128]{2,1,0:T(8,128)S(1)} %broadcast_in_dim.148), channel_id=1, replica_groups=mesh['zq'=4,'zp'=2,'yq'=2,'yp'=2,'xq'=2,'xp'=2,'rep'=2] {'zp','yp','xp'}, dimensions={0} | all-to-all | bytes 262144 | tf_op jit(solution)/shard_map/all_to_all | solution.py:45
  108.4 2.7 %collective-permute-start.24 = (bf16[544,128]{1,0:T(8,128)(2,1)S(1)}, bf16[544,128]{1,0:T(8,128)(2,1)S(1)}, u32[]{:S(2)}, u32[]{:S(2)}) collective-permute-start(bf16[544,128]{1,0:T(8,128)(2,1)S(1)} %get-tuple-element.71), channel_id=1, source_target_pairs={{0,4},{2,6},{4,0},{6,2},{8,12},{10,14},{12,8},{14,10},{16,20},{18,... | collective-permute-start | bytes 417800 | tf_op jit(solution)/shard_map/ppermute | solution.py:37
  111.1 3.1 %collective-permute-start.25 = (bf16[544,128]{1,0:T(8,128)(2,1)S(1)}, bf16[544,128]{1,0:T(8,128)(2,1)S(1)}, u32[]{:S(2)}, u32[]{:S(2)}) collective-permute-start(bf16[544,128]{1,0:T(8,128)(2,1)S(1)} %get-tuple-element.72), channel_id=1, source_target_pairs={{0,16},{2,18},{4,20},{6,22},{8,24},{10,26},{12,28},{14,30},{16,0},... | collective-permute-start | bytes 417800 | tf_op jit(solution)/shard_map/ppermute | solution.py:37
  115.5 4.5 %collective-permute-done.25.refs_2_ = bf16[544,128]{1,0:T(8,128)(2,1)S(1)} collective-permute-done((bf16[544,128]{1,0:T(8,128)(2,1)S(1)}, bf16[544,128]{1,0:T(8,128)(2,1)S(1)}, u32[]{:S(2)}, u32[]{:S(2)}) %collective-permute-start.25) | collective-permute-done | bytes 139296 | tf_op jit(solution)/shard_map/ppermute | solution.py:37
  120.0 3.1 %collective-permute-done.26.refs_3_ = bf16[544,128]{1,0:T(8,128)(2,1)S(1)} collective-permute-done((bf16[544,128]{1,0:T(8,128)(2,1)S(1)}, bf16[544,128]{1,0:T(8,128)(2,1)S(1)}, u32[]{:S(2)}, u32[]{:S(2)}) %collective-permute-start.26) | collective-permute-done | bytes 139296 | tf_op jit(solution)/shard_map/ppermute | solution.py:37
  123.2 4.7 %collective-permute-start.27 = (bf16[256,128]{1,0:T(8,128)(2,1)S(1)}, bf16[256,128]{1,0:T(8,128)(2,1)S(1)}, u32[]{:S(2)}, u32[]{:S(2)}) collective-permute-start(bf16[256,128]{1,0:T(8,128)(2,1)S(1)} %get-tuple-element.75), channel_id=1, source_target_pairs={{0,64},{2,66},{4,68},{6,70},{8,72},{10,74},{12,76},{14,78},{16,80}... | collective-permute-start | bytes 196616 | tf_op jit(solution)/shard_map/ppermute | solution.py:37
  129.1 2.5 %collective-permute-start.29 = (bf16[256,128]{1,0:T(8,128)(2,1)S(1)}, bf16[256,128]{1,0:T(8,128)(2,1)S(1)}, u32[]{:S(2)}, u32[]{:S(2)}) collective-permute-start(bf16[256,128]{1,0:T(8,128)(2,1)S(1)} %get-tuple-element.77), channel_id=1, source_target_pairs={{0,192},{2,194},{4,196},{6,198},{8,200},{10,202},{12,204},{14,206}... | collective-permute-start | bytes 196616 | tf_op jit(solution)/shard_map/ppermute | solution.py:37
  131.5 5.7 %collective-permute-done.28.refs_2_ = bf16[256,128]{1,0:T(8,128)(2,1)S(1)} collective-permute-done((bf16[256,128]{1,0:T(8,128)(2,1)S(1)}, bf16[256,128]{1,0:T(8,128)(2,1)S(1)}, u32[]{:S(2)}, u32[]{:S(2)}) %collective-permute-start.28) | collective-permute-done | bytes 65568 | tf_op jit(solution)/shard_map/ppermute | solution.py:37
  (86 shorter events, 40.1 us)
Async XLA Ops:
  0.6 15.0 %collective-permute-start = (bf16[1,128,128]{2,1,0:T(8,128)(2,1)}, bf16[1,128,128]{2,1,0:T(8,128)(2,1)S(1)}, u32[]{:S(2)}, u32[]{:S(2)}) collective-permute-start(bf16[1,128,128]{2,1,0:T(8,128)(2,1)} %bitcast.5), channel_id=1, source_target_pairs={{0,64},{2,66},{4,68},{6,70},{8,72},{10,74},{12,76},{14,78},{16,80}... | collective-permute-start | bytes 98312 | tf_op jit(solution)/shard_map/ppermute | solution.py:37
  4.0 11.7 %collective-permute-start.1 = (bf16[1,128,128]{2,1,0:T(8,128)(2,1)}, bf16[1,128,128]{2,1,0:T(8,128)(2,1)S(1)}, u32[]{:S(2)}, u32[]{:S(2)}) collective-permute-start(bf16[1,128,128]{2,1,0:T(8,128)(2,1)} %bitcast.6), channel_id=1, source_target_pairs={{0,128},{2,130},{4,132},{6,134},{8,136},{10,138},{12,140},{14,142}... | collective-permute-start | bytes 98312 | tf_op jit(solution)/shard_map/ppermute | solution.py:37
  8.5 7.2 %collective-permute-start.2 = (bf16[1,128,128]{2,1,0:T(8,128)(2,1)}, bf16[1,128,128]{2,1,0:T(8,128)(2,1)S(1)}, u32[]{:S(2)}, u32[]{:S(2)}) collective-permute-start(bf16[1,128,128]{2,1,0:T(8,128)(2,1)} %bitcast.7), channel_id=1, source_target_pairs={{0,192},{2,194},{4,196},{6,198},{8,200},{10,202},{12,204},{14,206}... | collective-permute-start | bytes 98312 | tf_op jit(solution)/shard_map/ppermute | solution.py:37
  22.8 8.9 %collective-permute-start.5 = (bf16[4,128,128]{2,1,0:T(8,128)(2,1)S(1)}, bf16[4,128,128]{2,1,0:T(8,128)(2,1)S(1)}, u32[]{:S(2)}, u32[]{:S(2)}) collective-permute-start(bf16[4,128,128]{2,1,0:T(8,128)(2,1)S(1)} %pad_maximum_fusion), channel_id=1, source_target_pairs={{0,20},{2,22},{4,16},{6,18},{8,28},{10,30},{12,24},{14,26},{16,4},... | collective-permute-start | bytes 393224 | tf_op jit(solution)/shard_map/ppermute | solution.py:37
  31.7 13.8 %collective-permute-start.6 = (bf16[16,128,128]{2,1,0:T(8,128)(2,1)S(1)}, bf16[16,128,128]{2,1,0:T(8,128)(2,1)S(1)}, u32[]{:S(2)}, u32[]{:S(2)}) collective-permute-start(bf16[16,128,128]{2,1,0:T(8,128)(2,1)S(1)} %constant_dynamic-update-slice_fusion.refs_0_), channel_id=1, source_target_pairs={{0,254},{2,248},{4,250},{6,252},{8,230},{10,224},{12,226},{14,228}... | collective-permute-start | bytes 1572872 | tf_op jit(solution)/shard_map/ppermute | solution.py:37
  33.8 14.9 %collective-permute-start.10 = (bf16[16,128,128]{2,1,0:T(8,128)(2,1)S(1)}, bf16[16,128,128]{2,1,0:T(8,128)(2,1)S(1)}, u32[]{:S(2)}, u32[]{:S(2)}) collective-permute-start(bf16[16,128,128]{2,1,0:T(8,128)(2,1)S(1)} %constant_dynamic-update-slice_fusion.refs_0_), channel_id=1, source_target_pairs={{0,2},{2,4},{4,6},{6,0},{8,10},{10,12},{12,14},{14,8},{16,18},{18,... | collective-permute-start | bytes 1572872 | tf_op jit(solution)/shard_map/ppermute | solution.py:37
  35.6 15.1 %collective-permute-start.11 = (bf16[16,128,128]{2,1,0:T(8,128)(2,1)S(1)}, bf16[16,128,128]{2,1,0:T(8,128)(2,1)S(1)}, u32[]{:S(2)}, u32[]{:S(2)}) collective-permute-start(bf16[16,128,128]{2,1,0:T(8,128)(2,1)S(1)} %constant_dynamic-update-slice_fusion.refs_0_), channel_id=1, source_target_pairs={{0,8},{2,10},{4,12},{6,14},{8,16},{10,18},{12,20},{14,22},{16,24},... | collective-permute-start | bytes 1572872 | tf_op jit(solution)/shard_map/ppermute | solution.py:37
  36.7 14.1 %collective-permute-start.12 = (bf16[16,128,128]{2,1,0:T(8,128)(2,1)S(1)}, bf16[16,128,128]{2,1,0:T(8,128)(2,1)S(1)}, u32[]{:S(2)}, u32[]{:S(2)}) collective-permute-start(bf16[16,128,128]{2,1,0:T(8,128)(2,1)S(1)} %constant_dynamic-update-slice_fusion.refs_0_), channel_id=1, source_target_pairs={{0,32},{2,34},{4,36},{6,38},{8,40},{10,42},{12,44},{14,46},{16,48}... | collective-permute-start | bytes 1572872 | tf_op jit(solution)/shard_map/ppermute | solution.py:37
  45.5 9.8 %collective-permute-start.7 = (bf16[16,128,128]{2,1,0:T(8,128)(2,1)S(1)}, bf16[16,128,128]{2,1,0:T(8,128)(2,1)S(1)}, u32[]{:S(2)}, u32[]{:S(2)}) collective-permute-start(bf16[16,128,128]{2,1,0:T(8,128)(2,1)S(1)} %collective-permute-done.6.refs_4_), channel_id=1, source_target_pairs={{0,224},{2,226},{4,228},{6,230},{8,232},{10,234},{12,236},{14,238}... | collective-permute-start | bytes 1572872 | tf_op jit(solution)/shard_map/ppermute | solution.py:37
  46.5 9.7 %collective-permute-start.8 = (bf16[16,128,128]{2,1,0:T(8,128)(2,1)S(1)}, bf16[16,128,128]{2,1,0:T(8,128)(2,1)S(1)}, u32[]{:S(2)}, u32[]{:S(2)}) collective-permute-start(bf16[16,128,128]{2,1,0:T(8,128)(2,1)S(1)} %collective-permute-done.6.refs_4_), channel_id=1, source_target_pairs={{0,24},{2,26},{4,28},{6,30},{8,0},{10,2},{12,4},{14,6},{16,8},{18,... | collective-permute-start | bytes 1572872 | tf_op jit(solution)/shard_map/ppermute | solution.py:37
  48.7 9.2 %collective-permute-start.9 = (bf16[16,128,128]{2,1,0:T(8,128)(2,1)S(1)}, bf16[16,128,128]{2,1,0:T(8,128)(2,1)S(1)}, u32[]{:S(2)}, u32[]{:S(2)}) collective-permute-start(bf16[16,128,128]{2,1,0:T(8,128)(2,1)S(1)} %collective-permute-done.6.refs_4_), channel_id=1, source_target_pairs={{0,6},{2,0},{4,2},{6,4},{8,14},{10,8},{12,10},{14,12},{16,22},{18,... | collective-permute-start | bytes 1572872 | tf_op jit(solution)/shard_map/ppermute | solution.py:37
  65.6 18.0 %collective-permute-start.20 = (bf16[16,128,128]{2,1,0:T(8,128)(2,1)S(1)}, bf16[16,128,128]{2,1,0:T(8,128)(2,1)S(1)}, u32[]{:S(2)}, u32[]{:S(2)}) collective-permute-start(bf16[16,128,128]{2,1,0:T(8,128)(2,1)S(1)} %get-tuple-element.67), channel_id=1, source_target_pairs={{0,224},{2,226},{4,228},{6,230},{8,232},{10,234},{12,236},{14,238}... | collective-permute-start | bytes 1572872 | tf_op jit(solution)/shard_map/ppermute | solution.py:37
  67.6 18.3 %collective-permute-start.21 = (bf16[16,128,128]{2,1,0:T(8,128)(2,1)}, bf16[16,128,128]{2,1,0:T(8,128)(2,1)S(1)}, u32[]{:S(2)}, u32[]{:S(2)}) collective-permute-start(bf16[16,128,128]{2,1,0:T(8,128)(2,1)} %get-tuple-element.68), channel_id=1, source_target_pairs={{0,24},{2,26},{4,28},{6,30},{8,0},{10,2},{12,4},{14,6},{16,8},{18,... | collective-permute-start | bytes 1572872 | tf_op jit(solution)/shard_map/ppermute | solution.py:37
  68.6 17.3 %collective-permute-start.22 = (bf16[16,128,128]{2,1,0:T(8,128)(2,1)}, bf16[16,128,128]{2,1,0:T(8,128)(2,1)}, u32[]{:S(2)}, u32[]{:S(2)}) collective-permute-start(bf16[16,128,128]{2,1,0:T(8,128)(2,1)} %get-tuple-element.69), channel_id=1, source_target_pairs={{0,6},{2,0},{4,2},{6,4},{8,14},{10,8},{12,10},{14,12},{16,22},{18,... | collective-permute-start | bytes 1572872 | tf_op jit(solution)/shard_map/ppermute | solution.py:37
  77.2 20.5 %all-to-all-start = ((f32[16,32,128]{2,1,0:T(8,128)}), f32[16,32,128]{2,1,0:T(8,128)S(1)}, u32[]{:S(2)}, u32[]{:S(2)}) async-start(f32[16,32,128]{2,1,0:T(8,128)} %bitcast.3), calls=%async_computation | async-start | bytes 524288 | tf_op jit(solution)/shard_map/all_to_all | solution.py:346
  82.5 25.4 %collective-permute-start.17 = (bf16[16,128,128]{2,1,0:T(8,128)(2,1)}, bf16[16,128,128]{2,1,0:T(8,128)(2,1)S(1)}, u32[]{:S(2)}, u32[]{:S(2)}) collective-permute-start(bf16[16,128,128]{2,1,0:T(8,128)(2,1)} %get-tuple-element.63), channel_id=1, source_target_pairs={{0,2},{2,4},{4,6},{6,0},{8,10},{10,12},{12,14},{14,8},{16,18},{18,... | collective-permute-start | bytes 1572872 | tf_op jit(solution)/shard_map/ppermute | solution.py:37
  82.9 25.1 %collective-permute-start.18 = (bf16[16,128,128]{2,1,0:T(8,128)(2,1)}, bf16[16,128,128]{2,1,0:T(8,128)(2,1)S(1)}, u32[]{:S(2)}, u32[]{:S(2)}) collective-permute-start(bf16[16,128,128]{2,1,0:T(8,128)(2,1)} %get-tuple-element.64), channel_id=1, source_target_pairs={{0,8},{2,10},{4,12},{6,14},{8,16},{10,18},{12,20},{14,22},{16,24},... | collective-permute-start | bytes 1572872 | tf_op jit(solution)/shard_map/ppermute | solution.py:37
  83.6 24.4 %collective-permute-start.19 = (bf16[16,128,128]{2,1,0:T(8,128)(2,1)}, bf16[16,128,128]{2,1,0:T(8,128)(2,1)S(1)}, u32[]{:S(2)}, u32[]{:S(2)}) collective-permute-start(bf16[16,128,128]{2,1,0:T(8,128)(2,1)} %copy-done.6), channel_id=1, source_target_pairs={{0,32},{2,34},{4,36},{6,38},{8,40},{10,42},{12,44},{14,46},{16,48}... | collective-permute-start | bytes 1572872 | tf_op jit(solution)/shard_map/ppermute | solution.py:37
  90.2 17.8 %collective-permute-start.23 = (bf16[16,128,128]{2,1,0:T(8,128)(2,1)}, bf16[16,128,128]{2,1,0:T(8,128)(2,1)S(1)}, u32[]{:S(2)}, u32[]{:S(2)}) collective-permute-start(bf16[16,128,128]{2,1,0:T(8,128)(2,1)} %class_sum.1), channel_id=1, source_target_pairs={{0,254},{2,248},{4,250},{6,252},{8,230},{10,224},{12,226},{14,228}... | collective-permute-start | bytes 1572872 | tf_op jit(solution)/shard_map/ppermute | solution.py:37
  111.1 8.9 %collective-permute-start.25 = (bf16[544,128]{1,0:T(8,128)(2,1)S(1)}, bf16[544,128]{1,0:T(8,128)(2,1)S(1)}, u32[]{:S(2)}, u32[]{:S(2)}) collective-permute-start(bf16[544,128]{1,0:T(8,128)(2,1)S(1)} %get-tuple-element.72), channel_id=1, source_target_pairs={{0,16},{2,18},{4,20},{6,22},{8,24},{10,26},{12,28},{14,30},{16,0},... | collective-permute-start | bytes 417800 | tf_op jit(solution)/shard_map/ppermute | solution.py:37
  114.2 9.0 %collective-permute-start.26 = (bf16[544,128]{1,0:T(8,128)(2,1)S(1)}, bf16[544,128]{1,0:T(8,128)(2,1)S(1)}, u32[]{:S(2)}, u32[]{:S(2)}) collective-permute-start(bf16[544,128]{1,0:T(8,128)(2,1)S(1)} %get-tuple-element.73), channel_id=1, source_target_pairs={{0,20},{2,22},{4,16},{6,18},{8,28},{10,30},{12,24},{14,26},{16,4},... | collective-permute-start | bytes 417800 | tf_op jit(solution)/shard_map/ppermute | solution.py:37
  123.2 8.3 %collective-permute-start.27 = (bf16[256,128]{1,0:T(8,128)(2,1)S(1)}, bf16[256,128]{1,0:T(8,128)(2,1)S(1)}, u32[]{:S(2)}, u32[]{:S(2)}) collective-permute-start(bf16[256,128]{1,0:T(8,128)(2,1)S(1)} %get-tuple-element.75), channel_id=1, source_target_pairs={{0,64},{2,66},{4,68},{6,70},{8,72},{10,74},{12,76},{14,78},{16,80}... | collective-permute-start | bytes 196616 | tf_op jit(solution)/shard_map/ppermute | solution.py:37
  127.9 9.4 %collective-permute-start.28 = (bf16[256,128]{1,0:T(8,128)(2,1)S(1)}, bf16[256,128]{1,0:T(8,128)(2,1)S(1)}, u32[]{:S(2)}, u32[]{:S(2)}) collective-permute-start(bf16[256,128]{1,0:T(8,128)(2,1)S(1)} %get-tuple-element.76), channel_id=1, source_target_pairs={{0,128},{2,130},{4,132},{6,134},{8,136},{10,138},{12,140},{14,142}... | collective-permute-start | bytes 196616 | tf_op jit(solution)/shard_map/ppermute | solution.py:37
  129.1 8.2 %collective-permute-start.29 = (bf16[256,128]{1,0:T(8,128)(2,1)S(1)}, bf16[256,128]{1,0:T(8,128)(2,1)S(1)}, u32[]{:S(2)}, u32[]{:S(2)}) collective-permute-start(bf16[256,128]{1,0:T(8,128)(2,1)S(1)} %get-tuple-element.77), channel_id=1, source_target_pairs={{0,192},{2,194},{4,196},{6,198},{8,200},{10,202},{12,204},{14,206}... | collective-permute-start | bytes 196616 | tf_op jit(solution)/shard_map/ppermute | solution.py:37
  (14 other events, 132.6 us)
